TPU v7x, 32 devices: a whole 2x2x4 slice. The times are simulated.
32 devices in a mesh: grp: 2 (over y), tm: 4 (over z), row: 2 (over x), col: 2 (over core).
Axes of the slice: x: 2, y: 2, z: 4, core: 2. Of those that a mesh axis runs over, the one named last changes fastest.
Arguments:
- frames: bfloat16 [8, 16, 9216], P(('grp', 'tm'), 'row', 'col'), parts along dimension 0, may hold values from -6 to 6
- owner_map: int32 [8], P('grp'), parts along dimension 0, may hold values from 0 to 3, each once
- valid_blocks: int32 [8, 2, 36], P(('grp', 'tm'), 'row', 'col'), parts along dimension 0, may hold values 0 or 1
- deblock_weight: bfloat16 [288, 32], replicated, may hold values from -0.375 to 0.375
- deblock_bias: float32 [32], replicated, may hold values from -3 to 3
- encoder_weight: bfloat16 [864, 64], replicated, may hold values from -0.21875 to 0.21875
- encoder_bias: float32 [64], replicated, may hold values from -3 to 3
Outputs:
- encoded: bfloat16 [6, 2, 4, 9216], P('grp', 'row', 'tm', 'col'), parts along dimension 0
There are 2 independent parts, one for each index of `grp`. A program takes and returns all parts, laid end to end along the dimension named above; an argument that names none is the same for every part. Nothing has to cross between parts.
Inputs may be any that keep to these rules, and one draw needn't show every extreme that they name: `owner_map`: each time index is held by exactly one slot.
All inputs are finite; a program needn't handle non-finite values. No bound on the sum of `valid_blocks` on one device may be relied on, other than what follows from the above.
Results may differ from a plain program's by a relative error of at most 0.0085.
Values may be sent and summed in bfloat16 or wider, within the bound.
A program may use at most 64 MiB of HBM per device.

v0:
```python
import jax
import jax.numpy as jnp
from jax import lax
from jax.sharding import PartitionSpec as P

CH = 32
OUTC = 64


def extended(cells, sides, width):
    for axis, dim in sides:
        count = lax.axis_size(axis)
        ends = count - 1
        head = lax.slice_in_dim(cells, 0, width, axis=dim)
        tail = lax.slice_in_dim(cells, cells.shape[dim] - width, cells.shape[dim], axis=dim)
        cells = jnp.concatenate(
            [
                lax.ppermute(tail, axis, [(i, (i + 1) % count) for i in range(ends)]),
                cells,
                lax.ppermute(head, axis, [((i + 1) % count, i) for i in range(ends)]),
            ],
            axis=dim,
        )
    return cells


def conv_taps(padded, weight, height, extent):
    channels = padded.shape[-1]
    summed = jnp.zeros((), jnp.float32)
    for row_step in range(3):
        stripe = padded[..., row_step : row_step + height, :, :]
        patches = jnp.concatenate(
            [stripe[..., col_step : col_step + extent, :] for col_step in range(3)], axis=-1
        )
        patches = patches.reshape(-1, 3 * channels)
        kernel = weight[row_step * 3 * channels : (row_step + 1) * 3 * channels]
        summed = summed + jnp.dot(patches, kernel, preferred_element_type=jnp.float32)
    return summed


def pool_pairs(source):
    leading = source.shape[:-3]
    height, extent, channels = source.shape[-3:]
    grouped = source.astype(jnp.float32).reshape(
        leading + (height // 2, 2, extent // 2, 2, channels)
    )
    depth = len(leading)
    return jnp.mean(grouped, axis=(depth + 1, depth + 3)).astype(jnp.bfloat16)


def regroup(stacked):
    return lax.all_to_all(stacked, "tm", split_axis=0, concat_axis=0, tiled=True)


def on_device(
    frames, owner_map, valid_blocks, deblock_weight, deblock_bias, encoder_weight, encoder_bias
):
    height = frames.shape[1]
    extent = frames.shape[2] // CH
    image = frames.reshape(height, extent, CH)
    framed = extended(image, (("row", 0), ("col", 1)), 1)
    filtered = (
        conv_taps(framed, deblock_weight, height, extent).reshape(height, extent, CH) + deblock_bias
    )
    blocks = valid_blocks[0].astype(jnp.float32)
    coverage = jnp.broadcast_to(blocks[:, None, :, None], (height // 8, 8, extent // 8, 8)).reshape(
        height, extent, 1
    )
    cleaned = (image.astype(jnp.float32) + coverage * filtered).astype(jnp.bfloat16)
    bands = lax.axis_size("tm")
    source = pool_pairs(cleaned)
    source_rows = source.shape[0]
    source_cols = source.shape[1]
    stride = source_rows // bands
    wide = extended(source, (("row", 0), ("col", 1)), 1)
    span = source_cols + 2
    upper = wide[:source_rows].reshape(bands, stride, span, CH)
    middle = wide[1 : 1 + source_rows].reshape(bands, stride, span, CH)
    lower = wide[2 : 2 + source_rows].reshape(bands, stride, span, CH)
    stacked = jnp.concatenate([upper, middle, lower], axis=1)
    arrived = regroup(stacked.reshape(bands, stride + 2, span * CH))
    ready = arrived.reshape(bands, stride + 2, span, CH)
    indices = jnp.arange(bands, dtype=jnp.int32)
    matches = (owner_map[None, :] == indices[:, None]).astype(jnp.int32)
    slot_of_time = jnp.sum(matches * indices[None, :], axis=1)
    ordered = jnp.take(ready, slot_of_time, axis=0)
    band_rows = ordered.shape[1] - 2
    band_cols = ordered.shape[2] - 2
    current = ordered[1:]
    previous = ordered[:-1]
    earlier = jnp.concatenate([ordered[:1], ordered[:-2]], axis=0)
    summed = encoder_bias
    for frame_lag, history in enumerate((current, previous, earlier)):
        kernel = encoder_weight[frame_lag * 9 * CH : (frame_lag + 1) * 9 * CH]
        summed = summed + conv_taps(history, kernel, band_rows, band_cols)
    encoded = summed.astype(jnp.bfloat16)
    return encoded.reshape(bands - 1, 1, band_rows, band_cols * OUTC)


def solution(mesh):
    return jax.shard_map(
        on_device,
        mesh=mesh,
        in_specs=(
            P(("grp", "tm"), "row", "col"),
            P("grp"),
            P(("grp", "tm"), "row", "col"),
            P(),
            P(),
            P(),
            P(),
        ),
        out_specs=P("grp", "row", "tm", "col"),
        check_vma=False,
    )
```

profile of v0, /device:TPU:0, one launch (start us, length us, event | category | flops | bytes accessed | tf_op | source)
XLA Modules:
  0.0 53.4 jit_solution(6096664387549325175)
XLA Ops:
  0.0 1.1 %slice_reduce_fusion = (bf16[4608]{0:T(1024)(128)(2,1)S(1)}, bf16[4608]{0:T(1024)(128)(2,1)S(1)}) fusion(bf16[1,8,4608]{2,1,0:T(8,128)(2,1)} %param.7), kind=kLoop, calls=%fused_computation.68 | loop fusion | bytes 36864 | tf_op jit(solution)/shard_map/slice | solution.py:14
  1.2 4.8 %collective-permute-start = (bf16[1,144,32]{2,1,0:T(8,128)(2,1)S(1)}, bf16[1,144,32]{2,1,0:T(8,128)(2,1)S(1)}, u32[]{:S(2)}, u32[]{:S(2)}) collective-permute-start(bf16[1,144,32]{2,1,0:T(8,128)(2,1)S(1)} %slice.267), channel_id=1, source_target_pairs={{0,2},{1,3},{4,6},{5,7},{8,10},{9,11},{12,14},{13,15},{16,18},{17,... | collective-permute-start | bytes 27656 | tf_op jit(solution)/shard_map/ppermute | solution.py:18
  6.2 1.3 %collective-permute-start.1 = (bf16[1,144,32]{2,1,0:T(8,128)(2,1)S(1)}, bf16[1,144,32]{2,1,0:T(8,128)(2,1)S(1)}, u32[]{:S(2)}, u32[]{:S(2)}) collective-permute-start(bf16[1,144,32]{2,1,0:T(8,128)(2,1)S(1)} %slice.269), channel_id=1, source_target_pairs={{2,0},{3,1},{6,4},{7,5},{10,8},{11,9},{14,12},{15,13},{18,16},{19,... | collective-permute-start | bytes 27656 | tf_op jit(solution)/shard_map/ppermute | solution.py:20
  7.9 4.1 %collective-permute-done.1 = bf16[1,144,32]{2,1,0:T(8,128)(2,1)S(1)} collective-permute-done((bf16[1,144,32]{2,1,0:T(8,128)(2,1)S(1)}, bf16[1,144,32]{2,1,0:T(8,128)(2,1)S(1)}, u32[]{:S(2)}, u32[]{:S(2)}) %collective-permute-start.1) | collective-permute-done | bytes 9248 | tf_op jit(solution)/shard_map/ppermute | solution.py:20
  12.2 1.3 %collective-permute-start.2 = (bf16[10,1,32]{1,2,0:T(8,128)(2,1)S(1)}, bf16[10,1,32]{1,2,0:T(8,128)(2,1)S(1)}, u32[]{:S(2)}, u32[]{:S(2)}) collective-permute-start(bf16[10,1,32]{1,2,0:T(8,128)(2,1)S(1)} %get-tuple-element.33), channel_id=1, source_target_pairs={{0,1},{2,3},{4,5},{6,7},{8,9},{10,11},{12,13},{14,15},{16,17},{18,... | collective-permute-start | bytes 1928 | tf_op jit(solution)/shard_map/ppermute | solution.py:18
  13.5 1.3 %collective-permute-start.3 = (bf16[10,1,32]{1,2,0:T(8,128)(2,1)S(1)}, bf16[10,1,32]{1,2,0:T(8,128)(2,1)S(1)}, u32[]{:S(2)}, u32[]{:S(2)}) collective-permute-start(bf16[10,1,32]{1,2,0:T(8,128)(2,1)S(1)} %get-tuple-element.34), channel_id=1, source_target_pairs={{1,0},{3,2},{5,4},{7,6},{9,8},{11,10},{13,12},{15,14},{17,16},{19,... | collective-permute-start | bytes 1928 | tf_op jit(solution)/shard_map/ppermute | solution.py:20
  15.8 0.9 %collective-permute-done.3 = bf16[10,1,32]{1,2,0:T(8,128)(2,1)S(1)} collective-permute-done((bf16[10,1,32]{1,2,0:T(8,128)(2,1)S(1)}, bf16[10,1,32]{1,2,0:T(8,128)(2,1)S(1)}, u32[]{:S(2)}, u32[]{:S(2)}) %collective-permute-start.3) | collective-permute-done | bytes 672 | tf_op jit(solution)/shard_map/ppermute | solution.py:20
  19.8 0.7 %copy-done.4 = f32[32]{0:T(128)S(1)} copy-done((f32[32]{0:T(128)S(1)}, f32[32]{0:T(128)}, u32[]{:S(2)}) %copy-start.4) | copy-done | bytes 152
  20.4 0.7 %convert_reduce_fusion = f32[4,72,32]{2,1,0:T(8,128)S(1)} fusion(f32[4,2,72,2,32]{4,3,2,1,0:T(2,128)S(1)} %reshape.135, f32[4,2,72,2,32]{4,3,2,1,0:T(2,128)S(1)} %bitcast.33, f32[32]{0:T(128)S(1)} %copy-done.4, f32[72]{0:T(128)S(1)} %broadcast_in_dim.25), kind=kLoop, calls=%fused_computation.13 | loop fusion | flops 211968 | bytes 332192 | tf_op jit(solution)/shard_map/reduce_sum | solution.py:48
  21.2 1.6 %collective-permute-start.4 = (bf16[1,72,32]{2,1,0:T(8,128)(2,1)S(1)}, bf16[1,72,32]{2,1,0:T(8,128)(2,1)S(1)}, u32[]{:S(2)}, u32[]{:S(2)}) collective-permute-start(bf16[1,72,32]{2,1,0:T(8,128)(2,1)S(1)} %get-tuple-element.45), channel_id=1, source_target_pairs={{0,2},{1,3},{4,6},{5,7},{8,10},{9,11},{12,14},{13,15},{16,18},{17,... | collective-permute-start | bytes 13832 | tf_op jit(solution)/shard_map/ppermute | solution.py:18
  22.8 1.3 %collective-permute-start.5 = (bf16[1,72,32]{2,1,0:T(8,128)(2,1)S(1)}, bf16[1,72,32]{2,1,0:T(8,128)(2,1)S(1)}, u32[]{:S(2)}, u32[]{:S(2)}) collective-permute-start(bf16[1,72,32]{2,1,0:T(8,128)(2,1)S(1)} %get-tuple-element.46), channel_id=1, source_target_pairs={{2,0},{3,1},{6,4},{7,5},{10,8},{11,9},{14,12},{15,13},{18,16},{19,... | collective-permute-start | bytes 13832 | tf_op jit(solution)/shard_map/ppermute | solution.py:20
  24.4 4.1 %collective-permute-done.5 = bf16[1,72,32]{2,1,0:T(8,128)(2,1)S(1)} collective-permute-done((bf16[1,72,32]{2,1,0:T(8,128)(2,1)S(1)}, bf16[1,72,32]{2,1,0:T(8,128)(2,1)S(1)}, u32[]{:S(2)}, u32[]{:S(2)}) %collective-permute-start.5) | collective-permute-done | bytes 4640 | tf_op jit(solution)/shard_map/ppermute | solution.py:20
  28.7 1.3 %collective-permute-start.6 = (bf16[6,1,32]{1,2,0:T(8,128)(2,1)S(1)}, bf16[6,1,32]{1,2,0:T(8,128)(2,1)S(1)}, u32[]{:S(2)}, u32[]{:S(2)}) collective-permute-start(bf16[6,1,32]{1,2,0:T(8,128)(2,1)S(1)} %get-tuple-element.50), channel_id=1, source_target_pairs={{0,1},{2,3},{4,5},{6,7},{8,9},{10,11},{12,13},{14,15},{16,17},{18,... | collective-permute-start | bytes 1160 | tf_op jit(solution)/shard_map/ppermute | solution.py:18
  30.0 1.3 %collective-permute-start.7 = (bf16[6,1,32]{1,2,0:T(8,128)(2,1)S(1)}, bf16[6,1,32]{1,2,0:T(8,128)(2,1)S(1)}, u32[]{:S(2)}, u32[]{:S(2)}) collective-permute-start(bf16[6,1,32]{1,2,0:T(8,128)(2,1)S(1)} %get-tuple-element.51), channel_id=1, source_target_pairs={{1,0},{3,2},{5,4},{7,6},{9,8},{11,10},{13,12},{15,14},{17,16},{19,... | collective-permute-start | bytes 1160 | tf_op jit(solution)/shard_map/ppermute | solution.py:20
  31.3 1.8 %collective-permute-done.7 = bf16[6,1,32]{1,2,0:T(8,128)(2,1)S(1)} collective-permute-done((bf16[6,1,32]{1,2,0:T(8,128)(2,1)S(1)}, bf16[6,1,32]{1,2,0:T(8,128)(2,1)S(1)}, u32[]{:S(2)}, u32[]{:S(2)}) %collective-permute-start.7) | collective-permute-done | bytes 416 | tf_op jit(solution)/shard_map/ppermute | solution.py:20
  34.1 0.7 %copy.96 = bf16[4,3,2368]{2,1,0:T(4,128)(2,1)} copy(bf16[4,3,2368]{2,0,1:T(4,128)(2,1)S(1)} %pad_maximum_fusion.7) | data formatting | bytes 113664 | tf_op jit(solution)/shard_map/concatenate | solution.py:80
  34.8 4.9 %all-to-all-start = ((bf16[4,3,2368]{2,1,0:T(4,128)(2,1)}), bf16[4,3,2368]{2,1,0:T(4,128)(2,1)S(1)}, u32[]{:S(2)}, u32[]{:S(2)}) async-start(bf16[4,3,2368]{2,1,0:T(4,128)(2,1)} %copy.96), calls=%async_computation | async-start | bytes 155648 | tf_op jit(solution)/shard_map/all_to_all | solution.py:52
  39.6 5.8 %all-to-all-done = bf16[4,3,2368]{2,1,0:T(4,128)(2,1)S(1)} async-done(((bf16[4,3,2368]{2,1,0:T(4,128)(2,1)}), bf16[4,3,2368]{2,1,0:T(4,128)(2,1)S(1)}, u32[]{:S(2)}, u32[]{:S(2)}) %all-to-all-start) | async-done | bytes 56864 | tf_op jit(solution)/shard_map/all_to_all | solution.py:52
  45.6 0.6 %gather_fusion = bf16[4,3,74,32]{3,2,1,0:T(8,128)(2,1)S(1)} fusion(bf16[4,3,74,32]{3,2,0,1:T(8,128)(2,1)S(1)} %reshape.124, s32[1024]{0:T(1024)S(1)} %pad_clamp_fusion), kind=kCustom, calls=%fused_computation | custom fusion | bytes 113680 | tf_op jit(solution)/shard_map/jit(_take)/gather | solution.py:86
  46.4 0.7 %copy-done = bf16[4,3,74,32]{3,2,1,0:T(8,128)(2,1)} copy-done((bf16[4,3,74,32]{3,2,1,0:T(8,128)(2,1)}, bf16[4,3,74,32]{3,2,1,0:T(8,128)(2,1)S(1)}, u32[]{:S(2)}) %copy-start) | copy-done | bytes 56856
  47.3 0.7 %slice-done = bf16[1,3,74,32]{3,2,1,0:T(8,128)(2,1)S(1)} async-done(((bf16[4,3,74,32]{3,2,1,0:T(8,128)(2,1)}), bf16[1,3,74,32]{3,2,1,0:T(8,128)(2,1)S(1)}, s32[]{:S(2)}) %slice-start) | async-done | bytes 14232 | tf_op jit(solution)/shard_map/slice | solution.py:91
  48.7 0.8 %copy-done.2 = bf16[864,64]{0,1:T(8,128)(2,1)S(1)} copy-done((bf16[864,64]{0,1:T(8,128)(2,1)S(1)}, bf16[864,64]{0,1:T(8,128)(2,1)}, u32[]{:S(2)}) %copy-start.2) | copy-done | bytes 110616
  51.3 0.6 %copy-done.5 = f32[64]{0:T(128)S(1)} copy-done((f32[64]{0:T(128)S(1)}, f32[64]{0:T(128)}, u32[]{:S(2)}) %copy-start.5) | copy-done | bytes 280
  52.6 0.7 %reshape.134 = bf16[3,1,1,4608]{3,0,2,1:T(4,128)(2,1)} reshape(bf16[216,64]{1,0:T(8,128)(2,1)S(1)} %copy.103) | data formatting | bytes 55296 | tf_op jit(solution)/shard_map/reshape | solution.py:97
  (91 shorter events, 9.9 us)
Async XLA Ops:
  0.0 7.5 %copy-start.1 = (bf16[1,8,4608]{2,1,0:T(8,128)(2,1)S(1)}, bf16[1,8,4608]{2,1,0:T(8,128)(2,1)}, u32[]{:S(2)}) copy-start(bf16[1,8,4608]{2,1,0:T(8,128)(2,1)} %param.7) | copy-start | bytes 221188
  1.2 6.6 %collective-permute-start = (bf16[1,144,32]{2,1,0:T(8,128)(2,1)S(1)}, bf16[1,144,32]{2,1,0:T(8,128)(2,1)S(1)}, u32[]{:S(2)}, u32[]{:S(2)}) collective-permute-start(bf16[1,144,32]{2,1,0:T(8,128)(2,1)S(1)} %slice.267), channel_id=1, source_target_pairs={{0,2},{1,3},{4,6},{5,7},{8,10},{9,11},{12,14},{13,15},{16,18},{17,... | collective-permute-start | bytes 27656 | tf_op jit(solution)/shard_map/ppermute | solution.py:18
  6.0 1.4 %copy-start.6 = (s32[1,1,18]{2,1,0:T(1,128)S(1)}, s32[1,1,18]{2,1,0:T(1,128)}, u32[]{:S(2)}) copy-start(s32[1,1,18]{2,1,0:T(1,128)} %param.9) | copy-start | bytes 220
  6.2 5.9 %collective-permute-start.1 = (bf16[1,144,32]{2,1,0:T(8,128)(2,1)S(1)}, bf16[1,144,32]{2,1,0:T(8,128)(2,1)S(1)}, u32[]{:S(2)}, u32[]{:S(2)}) collective-permute-start(bf16[1,144,32]{2,1,0:T(8,128)(2,1)S(1)} %slice.269), channel_id=1, source_target_pairs={{2,0},{3,1},{6,4},{7,5},{10,8},{11,9},{14,12},{15,13},{18,16},{19,... | collective-permute-start | bytes 27656 | tf_op jit(solution)/shard_map/ppermute | solution.py:20
  12.2 2.6 %copy-start.7 = (s32[4]{0:T(128)S(1)}, s32[4]{0:T(128)}, u32[]{:S(2)}) copy-start(s32[4]{0:T(128)} %param.8) | copy-start | bytes 52
  12.2 3.6 %collective-permute-start.2 = (bf16[10,1,32]{1,2,0:T(8,128)(2,1)S(1)}, bf16[10,1,32]{1,2,0:T(8,128)(2,1)S(1)}, u32[]{:S(2)}, u32[]{:S(2)}) collective-permute-start(bf16[10,1,32]{1,2,0:T(8,128)(2,1)S(1)} %get-tuple-element.33), channel_id=1, source_target_pairs={{0,1},{2,3},{4,5},{6,7},{8,9},{10,11},{12,13},{14,15},{16,17},{18,... | collective-permute-start | bytes 1928 | tf_op jit(solution)/shard_map/ppermute | solution.py:18
  13.5 3.2 %collective-permute-start.3 = (bf16[10,1,32]{1,2,0:T(8,128)(2,1)S(1)}, bf16[10,1,32]{1,2,0:T(8,128)(2,1)S(1)}, u32[]{:S(2)}, u32[]{:S(2)}) collective-permute-start(bf16[10,1,32]{1,2,0:T(8,128)(2,1)S(1)} %get-tuple-element.34), channel_id=1, source_target_pairs={{1,0},{3,2},{5,4},{7,6},{9,8},{11,10},{13,12},{15,14},{17,16},{19,... | collective-permute-start | bytes 1928 | tf_op jit(solution)/shard_map/ppermute | solution.py:20
  17.9 0.7 %copy-start.3 = (bf16[288,32]{0,1:T(8,128)(2,1)S(1)}, bf16[288,32]{0,1:T(8,128)(2,1)}, u32[]{:S(2)}) copy-start(bf16[288,32]{0,1:T(8,128)(2,1)} %param.10) | copy-start | bytes 55300
  19.8 0.7 %copy-start.4 = (f32[32]{0:T(128)S(1)}, f32[32]{0:T(128)}, u32[]{:S(2)}) copy-start(f32[32]{0:T(128)} %param.11) | copy-start | bytes 388
  21.2 3.1 %collective-permute-start.4 = (bf16[1,72,32]{2,1,0:T(8,128)(2,1)S(1)}, bf16[1,72,32]{2,1,0:T(8,128)(2,1)S(1)}, u32[]{:S(2)}, u32[]{:S(2)}) collective-permute-start(bf16[1,72,32]{2,1,0:T(8,128)(2,1)S(1)} %get-tuple-element.45), channel_id=1, source_target_pairs={{0,2},{1,3},{4,6},{5,7},{8,10},{9,11},{12,14},{13,15},{16,18},{17,... | collective-permute-start | bytes 13832 | tf_op jit(solution)/shard_map/ppermute | solution.py:18
  22.8 5.7 %collective-permute-start.5 = (bf16[1,72,32]{2,1,0:T(8,128)(2,1)S(1)}, bf16[1,72,32]{2,1,0:T(8,128)(2,1)S(1)}, u32[]{:S(2)}, u32[]{:S(2)}) collective-permute-start(bf16[1,72,32]{2,1,0:T(8,128)(2,1)S(1)} %get-tuple-element.46), channel_id=1, source_target_pairs={{2,0},{3,1},{6,4},{7,5},{10,8},{11,9},{14,12},{15,13},{18,16},{19,... | collective-permute-start | bytes 13832 | tf_op jit(solution)/shard_map/ppermute | solution.py:20
  28.7 2.6 %collective-permute-start.6 = (bf16[6,1,32]{1,2,0:T(8,128)(2,1)S(1)}, bf16[6,1,32]{1,2,0:T(8,128)(2,1)S(1)}, u32[]{:S(2)}, u32[]{:S(2)}) collective-permute-start(bf16[6,1,32]{1,2,0:T(8,128)(2,1)S(1)} %get-tuple-element.50), channel_id=1, source_target_pairs={{0,1},{2,3},{4,5},{6,7},{8,9},{10,11},{12,13},{14,15},{16,17},{18,... | collective-permute-start | bytes 1160 | tf_op jit(solution)/shard_map/ppermute | solution.py:18
  30.0 3.1 %collective-permute-start.7 = (bf16[6,1,32]{1,2,0:T(8,128)(2,1)S(1)}, bf16[6,1,32]{1,2,0:T(8,128)(2,1)S(1)}, u32[]{:S(2)}, u32[]{:S(2)}) collective-permute-start(bf16[6,1,32]{1,2,0:T(8,128)(2,1)S(1)} %get-tuple-element.51), channel_id=1, source_target_pairs={{1,0},{3,2},{5,4},{7,6},{9,8},{11,10},{13,12},{15,14},{17,16},{19,... | collective-permute-start | bytes 1160 | tf_op jit(solution)/shard_map/ppermute | solution.py:20
  34.8 10.6 %all-to-all-start = ((bf16[4,3,2368]{2,1,0:T(4,128)(2,1)}), bf16[4,3,2368]{2,1,0:T(4,128)(2,1)S(1)}, u32[]{:S(2)}, u32[]{:S(2)}) async-start(bf16[4,3,2368]{2,1,0:T(4,128)(2,1)} %copy.96), calls=%async_computation | async-start | bytes 155648 | tf_op jit(solution)/shard_map/all_to_all | solution.py:52
  46.3 0.7 %copy-start = (bf16[4,3,74,32]{3,2,1,0:T(8,128)(2,1)}, bf16[4,3,74,32]{3,2,1,0:T(8,128)(2,1)S(1)}, u32[]{:S(2)}) copy-start(bf16[4,3,74,32]{3,2,1,0:T(8,128)(2,1)S(1)} %broadcast_select_fusion) | copy-start | bytes 170500
  47.2 0.8 %slice-start = ((bf16[4,3,74,32]{3,2,1,0:T(8,128)(2,1)}), bf16[1,3,74,32]{3,2,1,0:T(8,128)(2,1)S(1)}, s32[]{:S(2)}) async-start(bf16[4,3,74,32]{3,2,1,0:T(8,128)(2,1)} %copy-done), calls=%async_computation.1 | async-start | bytes 122880 | tf_op jit(solution)/shard_map/slice | solution.py:91
  48.6 0.9 %copy-start.2 = (bf16[864,64]{0,1:T(8,128)(2,1)S(1)}, bf16[864,64]{0,1:T(8,128)(2,1)}, u32[]{:S(2)}) copy-start(bf16[864,64]{0,1:T(8,128)(2,1)} %param.12) | copy-start | bytes 331780
  51.3 0.7 %copy-start.5 = (f32[64]{0:T(128)S(1)}, f32[64]{0:T(128)}, u32[]{:S(2)}) copy-start(f32[64]{0:T(128)} %param.13) | copy-start | bytes 772
where the time goes:
time: 53.9 us; the launch traced here: 53.4 us
  starting transfers between devices  19.1 us (35%)
  waiting for transfers between devices  16.7 us (31%)
  local copies, waits for them, and re-layouts  12.2 us (23%)
  matrix products  2.47 us (5%)
  other arithmetic  2.43 us (5%)
    ppermute x4, waiting for transfers between devices, extended(): lax.ppermute(head, axis, [((i + 1) % count, i) for i in range(ends)])  10.9 us
    ppermute x4, starting transfers between devices, extended(): lax.ppermute(tail, axis, [(i, (i + 1) % count) for i in range(ends)])  9.04 us
    all_to_all x1, waiting for transfers between devices, regroup(): lax.all_to_all(stacked, 'tm', split_axis=0, concat_axis=0, tiled=True)  5.77 us
    ppermute x4, starting transfers between devices, extended(): lax.ppermute(head, axis, [((i + 1) % count, i) for i in range(ends)])  5.17 us
    all_to_all x1, starting transfers between devices, regroup(): lax.all_to_all(stacked, 'tm', split_axis=0, concat_axis=0, tiled=True)  4.87 us
    unnamed x16, local copies, waits for them, and re-layouts  3.24 us
    dot_general x12, matrix products, conv_taps(): jnp.dot(patches, kernel, preferred_element_type=jnp.float32)  2.47 us
    slice x2, local copies, waits for them, and re-layouts, extended(): head = lax.slice_in_dim(cells, 0, width, axis=dim)  1.19 us
  transfers between devices with their start and end apart: 9, of which 5 were waited for; matrix products, arithmetic and copies ran while one was open for 3% of the time, Pallas kernels for 0%

commit v1 on v0

v1 whole, which is shorter than its diff:
```python
import functools

import jax
import jax.numpy as jnp
from jax import lax
from jax.experimental import pallas as pl
from jax.experimental.pallas import tpu as pltpu
from jax.sharding import PartitionSpec as P

CH = 32
OUTC = 64
MESH = pl.DeviceIdType.MESH
F32 = jnp.float32
BF16 = jnp.bfloat16


def place(dr, dc):
    return (dr + 1) * 3 + dc + 1


DIRECTIONS = [(dr, dc) for dr in (-1, 0, 1) for dc in (-1, 0, 1) if (dr, dc) != (0, 0)]


def iota(shape, dim):
    return lax.broadcasted_iota(jnp.int32, shape, dim)


def spread_taps(taps, spread):
    return lax.dot_general(taps, spread, (((0,), (0,)), ((), ())), preferred_element_type=F32)


def deblock_matrix(dw_ref, t_ref):
    spread = (iota((CH, 4 * CH), 1) % CH == iota((CH, 4 * CH), 0)).astype(BF16)
    tiled = spread_taps(dw_ref[...], spread)
    taps = [[tiled[(3 * a + b) * CH : (3 * a + b + 1) * CH] for b in range(3)] for a in range(3)]
    wide = [
        [sum(row[b] for b in (d - 1, d) if 0 <= b < 3) for d in range(4)]
        for row in taps
    ]
    four = [
        [0.25 * sum(wide[a][d] for a in (e - 1, e) if 0 <= a < 3) for d in range(4)]
        for e in range(4)
    ]
    block = iota((CH, 4 * CH), 1) // CH
    zero = jnp.zeros((CH, 4 * CH), F32)
    rows, cols = iota((8 * CH, 4 * CH), 0), iota((8 * CH, 4 * CH), 1)
    mean = jnp.where((rows // (2 * CH) == cols // CH) & (rows % CH == cols % CH), 0.25, 0.0).astype(BF16)
    nothing = jnp.zeros((8 * CH, 4 * CH), BF16)
    for e in range(4):
        base = e * 12 * CH

        def put(at, pixel):
            total = zero
            for o in range(4):
                d = pixel - 2 * o + 1
                if 0 <= d < 4:
                    total = jnp.where(block == o, four[e][d], total)
            t_ref[base + at * CH : base + (at + 1) * CH, : 4 * CH] = total.astype(BF16)

        for pixel in range(8):
            put(pixel, pixel)
        put(8, 8)
        put(11, -1)
        t_ref[base + 9 * CH : base + 11 * CH, : 4 * CH] = nothing[: 2 * CH]
        t_ref[base : base + 8 * CH, 4 * CH :] = mean if e in (1, 2) else nothing
        t_ref[base + 8 * CH : base + 12 * CH, 4 * CH :] = nothing[: 4 * CH]


def encoder_matrix(ew_ref, t_ref):
    width = 4 * OUTC
    spread = (iota((OUTC, width), 1) % OUTC == iota((OUTC, width), 0)).astype(BF16)
    block = iota((CH, width), 1) // OUTC
    zero = jnp.zeros((CH, width), F32)
    nothing = jnp.zeros((2 * CH, width), BF16)
    everything = spread_taps(ew_ref[...], spread)
    for lag in range(3):
        tiled = everything[lag * 9 * CH : (lag + 1) * 9 * CH]
        for dy in range(3):
            base = dy * 8 * CH
            left = lag * width

            def put(at, pixel):
                total = zero
                for o in range(4):
                    d = pixel - o + 1
                    if 0 <= d < 3:
                        tap = tiled[(3 * dy + d) * CH : (3 * dy + d + 1) * CH]
                        total = jnp.where(block == o, tap, total)
                t_ref[base + at * CH : base + (at + 1) * CH, left : left + width] = total.astype(BF16)

            for pixel in range(4):
                put(pixel, pixel)
            put(4, 4)
            put(7, -1)
            t_ref[base + 5 * CH : base + 7 * CH, left : left + width] = nothing


def kernel(
    sizes,
    owner_ref,
    raw_ref,
    x_ref,
    vb_ref,
    dw_ref,
    db_ref,
    ew_ref,
    eb_ref,
    out_ref,
    ext,
    halo,
    edge,
    flags,
    tdeb,
    tenc,
    pooled,
    bands_in,
    product,
    send_sem,
    recv_sem,
    band_send,
    band_recv,
):
    n, nr, nc = sizes
    height, groups, _ = x_ref.shape
    padded = ext.shape[1]
    half = height // 2
    stride = half // n
    me = lax.axis_index("tm")
    r = lax.axis_index("row")
    c = lax.axis_index("col")

    halo[...] = jnp.zeros_like(halo)
    edge[...] = jnp.zeros_like(edge)
    flags[...] = jnp.zeros_like(flags)

    def exists(dr, dc):
        found = None
        for step, at, count in ((dr, r, nr), (dc, c, nc)):
            if step:
                inside = at > 0 if step < 0 else at < count - 1
                found = inside if found is None else jnp.logical_and(found, inside)
        return found

    def copies(dr, dc):
        here, there = place(dr, dc), place(-dr, -dc)
        to = {}
        if dr:
            to["row"] = r + dr
        if dc:
            to["col"] = c + dc
        if dc:
            lanes = pl.ds(0, 4 * CH) if dc < 0 else pl.ds(raw_ref.shape[1] - 4 * CH, 4 * CH)
            src, dst = raw_ref.at[:, lanes], edge.at[there]
        else:
            src = x_ref.at[pl.ds(0 if dr < 0 else height - 3, 3)]
            dst = halo.at[1 if dr < 0 else 0]
        return [
            pltpu.make_async_remote_copy(
                src_ref=a, dst_ref=b, send_sem=send_sem.at[here, k], recv_sem=recv_sem.at[there, k],
                device_id=to, device_id_type=MESH,
            )
            for k, (a, b) in enumerate(((src, dst), (vb_ref, flags.at[there])))
        ]

    barrier = pltpu.get_barrier_semaphore()
    for dr, dc in DIRECTIONS:
        to = {}
        if dr:
            to["row"] = r + dr
        if dc:
            to["col"] = c + dc

        @pl.when(exists(dr, dc))
        def _():
            pl.semaphore_signal(barrier, inc=1, device_id=to, device_id_type=MESH)

    for d in range(1, n):
        pl.semaphore_signal(
            barrier, inc=1, device_id={"tm": lax.rem(me + d, n)}, device_id_type=MESH
        )
    tall = (r > 0).astype(jnp.int32) + (r < nr - 1).astype(jnp.int32) + 1
    broad = (c > 0).astype(jnp.int32) + (c < nc - 1).astype(jnp.int32) + 1
    pl.semaphore_wait(barrier, tall * broad - 1 + n - 1)

    for dr, dc in DIRECTIONS:

        @pl.when(exists(dr, dc))
        def _():
            for copy in copies(dr, dc):
                copy.start()

    deblock_matrix(dw_ref, tdeb)
    ext[...] = jnp.zeros_like(ext)
    ext[3 : 3 + height, :groups, : 8 * CH] = x_ref[...].astype(F32)

    for dr, dc in DIRECTIONS:

        @pl.when(exists(dr, dc))
        def _():
            for copy in copies(-dr, -dc):
                copy.wait_recv()

    ext[:3, :groups, : 8 * CH] = halo[0].astype(F32)
    ext[3 + height :, :groups, : 8 * CH] = halo[1].astype(F32)
    for dc, at, lanes in ((-1, padded - 1, 4 * CH), (1, groups, 0)):
        middle = edge[place(0, dc)].astype(F32)
        top = edge[place(-1, dc)].astype(F32)
        low = edge[place(1, dc)].astype(F32)
        lines = [top[height - 3 + k : height - 2 + k] for k in range(3)]
        lines += [middle[k : k + 1] for k in range(height)]
        lines += [low[k : k + 1] for k in range(3)]
        for k, line in enumerate(lines):
            ext[k, at : at + 1, lanes : lanes + 4 * CH] = line

    lane = iota((padded, 4 * CH), 1)
    for k in range(height + 6):
        before = pltpu.roll(ext[k, :, 4 * CH : 8 * CH], 1, 0)
        after = pltpu.roll(ext[k, :, : 4 * CH], padded - 1, 0)
        ext[k, :, 8 * CH :] = jnp.where(
            lane >= 3 * CH, before, jnp.where(lane < CH, after, 0.0)
        )

    lhs = jnp.concatenate(
        [
            jnp.concatenate([ext[2 * k + e] for e in range(4)], axis=1)
            for k in range(half + 2)
        ],
        axis=0,
    ).astype(BF16)
    conv = jnp.dot(lhs, tdeb[...], preferred_element_type=F32)

    def column(line, left, right):
        spot = iota((padded, groups), 0)
        own = jnp.sum(
            jnp.where(spot == iota((padded, groups), 1), jnp.broadcast_to(line, (padded, groups)), 0.0),
            axis=1, keepdims=True,
        )
        spot = iota((padded, 1), 0)
        own = jnp.where(spot == padded - 1, jnp.broadcast_to(left[:, groups - 1 :], (padded, 1)), own)
        return jnp.where(spot == groups, jnp.broadcast_to(right[:, :1], (padded, 1)), own)

    blocks = vb_ref.shape[0]

    def flag_row(dr, k):
        rows = [
            vb_ref[k : k + 1, :] if (dr, dc) == (0, 0) else flags[place(dr, dc), k : k + 1, :]
            for dc in (-1, 0, 1)
        ]
        left, line, right = [row.astype(F32) for row in rows]
        return column(line, left, right)

    masks = [flag_row(-1, blocks - 1)] + [flag_row(0, k) for k in range(blocks)] + [flag_row(1, 0)]
    deblock_bias = jnp.concatenate([db_ref[...]] * 4, axis=1)
    per = half // blocks
    for k in range(half + 2):
        part = conv[k * padded : (k + 1) * padded]
        which = 0 if k == 0 else blocks + 1 if k == half + 1 else 1 + (k - 1) // per
        pooled[k] = (
            part[:, 4 * CH :] + masks[which] * (part[:, : 4 * CH] + deblock_bias)
        ).astype(BF16)

    def band_copy(d):
        to = lax.rem(me + d, n)
        return pltpu.make_async_remote_copy(
            src_ref=pooled.at[pl.ds(to * stride, stride + 2)],
            dst_ref=bands_in.at[me],
            send_sem=band_send.at[d],
            recv_sem=band_recv.at[d],
            device_id={"tm": to},
            device_id_type=MESH,
        )

    def band_arrival(d):
        source = lax.rem(me + n - d, n)
        return pltpu.make_async_remote_copy(
            src_ref=pooled.at[pl.ds(0, stride + 2)],
            dst_ref=bands_in.at[source],
            send_sem=band_send.at[d],
            recv_sem=band_recv.at[d],
            device_id={"tm": source},
            device_id_type=MESH,
        )

    for d in range(1, n):
        band_copy(d).start()
    bands_in[me] = pooled[pl.ds(me * stride, stride + 2)]
    encoder_matrix(ew_ref, tenc)
    for d in range(1, n):
        band_arrival(d).wait_recv()

    rows = []
    for s in range(n):
        lines = []
        for k in range(stride + 2):
            own = bands_in[s, k].astype(F32)
            side = jnp.where(
                lane >= 3 * CH,
                pltpu.roll(own, 1, 0),
                jnp.where(lane < CH, pltpu.roll(own, padded - 1, 0), 0.0),
            )
            lines.append(jnp.concatenate([own, side], axis=1))
        for k in range(stride):
            rows.append(jnp.concatenate(lines[k : k + 3], axis=1))
    lhs = jnp.concatenate(rows, axis=0).astype(BF16)
    found = jnp.dot(lhs, tenc[...], preferred_element_type=F32)
    product[...] = found.reshape(product.shape)

    slots = []
    for t in range(n):
        if n <= 8:
            slot = jnp.int32(0)
            for s in range(n):
                slot = jnp.where(owner_ref[s] == t, s, slot)
        else:
            slot = lax.fori_loop(
                0, n, lambda s, held: jnp.where(owner_ref[s] == t, s, held), jnp.int32(0)
            )
        slots.append(slot)
    width = 4 * OUTC
    encoder_bias = jnp.concatenate([eb_ref[...]] * 4, axis=1)
    for t in range(1, n):
        for k in range(stride):
            total = encoder_bias
            for lag in range(3):
                total = total + product[slots[max(t - lag, 0)], k, :, lag * width : (lag + 1) * width]
            out_ref[t - 1, k] = total[:groups].astype(BF16)

    for dr, dc in DIRECTIONS:

        @pl.when(exists(dr, dc))
        def _():
            for copy in copies(dr, dc):
                copy.wait_send()

    for d in range(1, n):
        band_copy(d).wait_send()


def on_device(
    sizes, frames, owner_map, valid_blocks, deblock_weight, deblock_bias, encoder_weight, encoder_bias
):
    n = sizes[0]
    _, height, lanes = frames.shape
    raw = frames[0]
    groups = lanes // (8 * CH)
    padded = -(-(groups + 2) // 8) * 8
    blocks = valid_blocks.shape[1]
    half = height // 2
    stride = half // n
    x = raw.reshape(height, groups, 8 * CH)
    vmem = pl.BlockSpec(memory_space=pltpu.VMEM)
    encoded = pl.pallas_call(
        functools.partial(kernel, sizes),
        out_shape=jax.ShapeDtypeStruct((n - 1, stride, groups, 4 * OUTC), BF16),
        in_specs=[pl.BlockSpec(memory_space=pltpu.SMEM), pl.BlockSpec(memory_space=pl.ANY)] + [vmem] * 6,
        out_specs=vmem,
        scratch_shapes=[
            pltpu.VMEM((height + 6, padded, 12 * CH), F32),
            pltpu.VMEM((2, 3, groups, 8 * CH), BF16),
            pltpu.VMEM((9, height, 4 * CH), BF16),
            pltpu.VMEM((9, blocks, groups), jnp.int32),
            pltpu.VMEM((48 * CH, 8 * CH), BF16),
            pltpu.VMEM((24 * CH, 12 * OUTC), BF16),
            pltpu.VMEM((half + 2, padded, 4 * CH), BF16),
            pltpu.VMEM((n, stride + 2, padded, 4 * CH), BF16),
            pltpu.VMEM((n, stride, padded, 12 * OUTC), F32),
            pltpu.SemaphoreType.DMA((9, 2)),
            pltpu.SemaphoreType.DMA((9, 2)),
            pltpu.SemaphoreType.DMA((n,)),
            pltpu.SemaphoreType.DMA((n,)),
        ],
        compiler_params=pltpu.CompilerParams(
            collective_id=0, has_side_effects=True, vmem_limit_bytes=40 * 1024 * 1024
        ),
    )(
        owner_map, raw, x, valid_blocks[0], deblock_weight.T, deblock_bias[None], encoder_weight.T,
        encoder_bias[None],
    )
    return encoded.reshape(n - 1, 1, stride, groups * 4 * OUTC)


def solution(mesh):
    sizes = (mesh.shape["tm"], mesh.shape["row"], mesh.shape["col"])
    return jax.shard_map(
        functools.partial(on_device, sizes),
        mesh=mesh,
        in_specs=(
            P(("grp", "tm"), "row", "col"),
            P("grp"),
            P(("grp", "tm"), "row", "col"),
            P(),
            P(),
            P(),
            P(),
        ),
        out_specs=P("grp", "row", "tm", "col"),
        check_vma=False,
    )
```

time: 53.9 us -> 15.9 us (0.29)
  starting transfers between devices: 19.1 us -> 0 us
  waiting for transfers between devices: 16.7 us -> 0 us
  Pallas kernels: 0 us -> 13.1 us
  local copies, waits for them, and re-layouts: 12.2 us -> 2.55 us
  matrix products: 2.47 us -> 0 us
  other arithmetic: 2.43 us -> 0 us
    ppermute x8 -> x0, starting transfers between devices: 14.2 us -> none  [the longest x4 9.04 us: extended(): lax.ppermute(tail, axis, [(i, (i + 1) % count) for i in range(ends)])]
    pallas_call x0 -> x1, Pallas kernels: none -> 13.1 us  [on_device(): pl.pallas_call(functools.partial(kernel, sizes), out_shape=jax.ShapeDtype...]
    ppermute x8 -> x0, waiting for transfers between devices: 10.9 us -> none  [the longest x4 10.9 us: extended(): lax.ppermute(head, axis, [((i + 1) % count, i) for i in range(ends)])]
    all_to_all x1 -> x0, waiting for transfers between devices: 5.77 us -> none  [regroup(): lax.all_to_all(stacked, 'tm', split_axis=0, concat_axis=0, tiled=True)]
    all_to_all x1 -> x0, starting transfers between devices: 4.87 us -> none  [regroup(): lax.all_to_all(stacked, 'tm', split_axis=0, concat_axis=0, tiled=True)]
    slice x19 -> x0, local copies, waits for them, and re-layouts: 3.58 us -> none  [the longest x2 1.19 us: extended(): head = lax.slice_in_dim(cells, 0, width, axis=dim)]
    dot_general x12 -> x0, matrix products: 2.47 us -> none  [conv_taps(): jnp.dot(patches, kernel, preferred_element_type=jnp.float32)]
    unnamed x16 -> x14, local copies, waits for them, and re-layouts: 3.24 us -> 0.92 us
  transfers between devices with their start and end apart: 9 -> 0, of which waited for: 5 -> 0; matrix products, arithmetic and copies ran while one was open for 3% -> 0% of each run, Pallas kernels for 0% -> 0%
where the time goes in v1:
time: 15.9 us; the launch traced here: 15.8 us
  Pallas kernels  13.1 us (82%)
  local copies, waits for them, and re-layouts  2.55 us (16%)
    pallas_call x1, Pallas kernels, on_device(): pl.pallas_call(functools.partial(kernel, sizes), out_shape=jax.ShapeDtype...  13.1 us
    another operation x1, local copies, waits for them, and re-layouts, on_device(): x = raw.reshape(height, groups, 8 * CH)  0.99 us
    unnamed x14, local copies, waits for them, and re-layouts  0.92 us
    reshape x1, local copies, waits for them, and re-layouts, on_device(): return encoded.reshape(n - 1, 1, stride, groups * 4 * OUTC)  0.64 us

profile of v1, /device:TPU:0, one launch (start us, length us, event | category | flops | bytes accessed | tf_op | source)
XLA Modules:
  0.0 15.8 jit_solution(12931408438731718523)
XLA Ops:
  0.0 0.0 copy-start
  0.0 0.0 copy-start.2
  0.0 0.0 copy-start.3
  0.0 0.0 copy-start.4
  0.0 0.0 copy-start.5
  0.0 0.0 copy-start.6
  0.0 1.0 %copy.8.x_ref = bf16[8,18,256]{2,1,0:T(8,128)(2,1)S(1)} copy(bf16[8,18,256]{2,0,1:T(8,128)(2,1)} %bitcast.7) | data formatting | bytes 147456 | tf_op jit(solution)/shard_map/reshape;squeeze | solution.py:350
  1.0 0.0 copy-done
  1.0 0.0 copy-done.2
  1.0 0.0 copy-done.3
  1.0 0.0 copy-done.4
  1.1 0.0 copy-done.5
  1.1 0.0 copy-done.6
  1.1 0.0 copy-start.1
  1.1 0.9 %copy-done.1 = bf16[864,64]{0,1:T(8,128)(2,1)S(1)} copy-done((bf16[864,64]{0,1:T(8,128)(2,1)S(1)}, bf16[864,64]{0,1:T(8,128)(2,1)}, u32[]{:S(2)}) %copy-start.1) | copy-done | bytes 110616
  2.0 13.1 %shard_map.73 = bf16[3,1,18,256]{3,2,1,0:T(8,128)(2,1)S(1)} custom-call(s32[4]{0:T(128)S(1)} %copy-done.3, bf16[8,4608]{1,0:T(8,128)(2,1)S(1)} %bitcast.8, bf16[8,18,256]{2,1,0:T(8,128)(2,1)S(1)} %copy.8.x_ref, s32[1,18]{1,0:T(1,128)S(1)} %bitcast.11, bf16[32,288]{1,0:T(8,128)(2,1)S(1)} %bitcast.10, f32[1,32]{1,0:T(1,128)S(1)} %bitcast.12, ...), custom_call_target="tpu_custom_call" | custom-call | tf_op jit(solution)/shard_map/pallas_call | solution.py:352
  15.1 0.6 %reshape.3 = bf16[3,1,1,4608]{3,0,2,1:T(4,128)(2,1)} reshape(bf16[3,1,18,256]{3,2,1,0:T(8,128)(2,1)S(1)} %shard_map.73) | data formatting | bytes 55296 | tf_op jit(solution)/shard_map/reshape | solution.py:379
Async XLA Ops:
  0.0 1.0 %copy-start = (bf16[1,8,4608]{2,1,0:T(8,128)(2,1)S(1)}, bf16[1,8,4608]{2,1,0:T(8,128)(2,1)}, u32[]{:S(2)}) copy-start(bf16[1,8,4608]{2,1,0:T(8,128)(2,1)} %param.7) | copy-start | bytes 221188
  0.0 1.0 %copy-start.2 = (bf16[288,32]{0,1:T(8,128)(2,1)S(1)}, bf16[288,32]{0,1:T(8,128)(2,1)}, u32[]{:S(2)}) copy-start(bf16[288,32]{0,1:T(8,128)(2,1)} %param.10) | copy-start | bytes 55300
  0.0 1.0 %copy-start.3 = (s32[4]{0:T(128)S(1)}, s32[4]{0:T(128)}, u32[]{:S(2)}) copy-start(s32[4]{0:T(128)} %owner_ref.1) | copy-start | bytes 52
  0.0 1.0 %copy-start.4 = (s32[1,1,18]{2,1,0:T(1,128)S(1)}, s32[1,1,18]{2,1,0:T(1,128)}, u32[]{:S(2)}) copy-start(s32[1,1,18]{2,1,0:T(1,128)} %param.9) | copy-start | bytes 220
  0.0 1.1 %copy-start.5 = (f32[32]{0:T(128)S(1)}, f32[32]{0:T(128)}, u32[]{:S(2)}) copy-start(f32[32]{0:T(128)} %param.11) | copy-start | bytes 388
  0.0 1.1 %copy-start.6 = (f32[64]{0:T(128)S(1)}, f32[64]{0:T(128)}, u32[]{:S(2)}) copy-start(f32[64]{0:T(128)} %param.13) | copy-start | bytes 772
  1.1 0.9 %copy-start.1 = (bf16[864,64]{0,1:T(8,128)(2,1)S(1)}, bf16[864,64]{0,1:T(8,128)(2,1)}, u32[]{:S(2)}) copy-start(bf16[864,64]{0,1:T(8,128)(2,1)} %param.12) | copy-start | bytes 331780

commit v2 on v1

--- a/solution.py
+++ b/solution.py
@@ -97,16 +97,23 @@
 
 def kernel(
     sizes,
+    owner_hbm,
+    raw_hbm,
+    vb_hbm,
+    dw_hbm,
+    db_hbm,
+    ew_hbm,
+    eb_hbm,
+    out_ref,
     owner_ref,
     raw_ref,
-    x_ref,
     vb_ref,
     dw_ref,
     db_ref,
     ew_ref,
     eb_ref,
-    out_ref,
     ext,
+    outgoing,
     halo,
     edge,
     flags,
@@ -115,19 +122,38 @@
     pooled,
     bands_in,
     product,
+    load_sem,
     send_sem,
     recv_sem,
     band_send,
     band_recv,
 ):
     n, nr, nc = sizes
-    height, groups, _ = x_ref.shape
-    padded = ext.shape[1]
+    height, width = raw_ref.shape
+    groups = width // (8 * CH)
+    padded = halo.shape[2]
     half = height // 2
     stride = half // n
     me = lax.axis_index("tm")
     r = lax.axis_index("row")
     c = lax.axis_index("col")
+
+    loads = [
+        pltpu.make_async_copy(a, b, load_sem.at[k])
+        for k, (a, b) in enumerate(
+            (
+                (raw_hbm, raw_ref),
+                (vb_hbm, vb_ref),
+                (dw_hbm, dw_ref),
+                (db_hbm, db_ref),
+                (ew_hbm, ew_ref),
+                (eb_hbm, eb_ref),
+                (owner_hbm, owner_ref),
+            )
+        )
+    ]
+    for load in loads:
+        load.start()
 
     halo[...] = jnp.zeros_like(halo)
     edge[...] = jnp.zeros_like(edge)
@@ -152,7 +178,7 @@
             lanes = pl.ds(0, 4 * CH) if dc < 0 else pl.ds(raw_ref.shape[1] - 4 * CH, 4 * CH)
             src, dst = raw_ref.at[:, lanes], edge.at[there]
         else:
-            src = x_ref.at[pl.ds(0 if dr < 0 else height - 3, 3)]
+            src = outgoing.at[0 if dr < 0 else 1]
             dst = halo.at[1 if dr < 0 else 0]
         return [
             pltpu.make_async_remote_copy(
@@ -178,6 +204,27 @@
         pl.semaphore_signal(
             barrier, inc=1, device_id={"tm": lax.rem(me + d, n)}, device_id_type=MESH
         )
+    ext[...] = jnp.zeros_like(ext)
+
+    def line_of(k):
+        return pl.ds(k * padded, padded)
+
+    loads[0].wait()
+    for h in range(0, height, 8):
+        for q in range(2 * groups):
+            ext[q % 2, pl.ds((3 + h) * padded + q // 2, 8, stride=padded), :] = raw_ref[
+                h : h + 8, q * 4 * CH : (q + 1) * 4 * CH
+            ].astype(F32)
+    for side, dr in enumerate((-1, 1)):
+
+        @pl.when(exists(dr, 0))
+        def _():
+            for k in range(3):
+                line = line_of(3 + k if dr < 0 else height + k)
+                for j in range(2):
+                    outgoing[side, k, :, j * 4 * CH : (j + 1) * 4 * CH] = ext[j, line, :].astype(BF16)
+
+    loads[1].wait()
     tall = (r > 0).astype(jnp.int32) + (r < nr - 1).astype(jnp.int32) + 1
     broad = (c > 0).astype(jnp.int32) + (c < nc - 1).astype(jnp.int32) + 1
     pl.semaphore_wait(barrier, tall * broad - 1 + n - 1)
@@ -189,9 +236,9 @@
             for copy in copies(dr, dc):
                 copy.start()
 
+    loads[2].wait()
+    loads[3].wait()
     deblock_matrix(dw_ref, tdeb)
-    ext[...] = jnp.zeros_like(ext)
-    ext[3 : 3 + height, :groups, : 8 * CH] = x_ref[...].astype(F32)
 
     for dr, dc in DIRECTIONS:
 
@@ -200,29 +247,34 @@
             for copy in copies(-dr, -dc):
                 copy.wait_recv()
 
-    ext[:3, :groups, : 8 * CH] = halo[0].astype(F32)
-    ext[3 + height :, :groups, : 8 * CH] = halo[1].astype(F32)
-    for dc, at, lanes in ((-1, padded - 1, 4 * CH), (1, groups, 0)):
-        middle = edge[place(0, dc)].astype(F32)
+    for side, first in ((0, 0), (1, 3 + height)):
+        for k in range(3):
+            for j in range(2):
+                ext[j, line_of(first + k), :] = halo[
+                    side, k, :, j * 4 * CH : (j + 1) * 4 * CH
+                ].astype(F32)
+    for dc, at, j in ((-1, padded - 1, 1), (1, groups, 0)):
+        for h in range(0, height, 8):
+            ext[j, pl.ds((3 + h) * padded + at, 8, stride=padded), :] = edge[
+                place(0, dc), h : h + 8
+            ].astype(F32)
         top = edge[place(-1, dc)].astype(F32)
         low = edge[place(1, dc)].astype(F32)
-        lines = [top[height - 3 + k : height - 2 + k] for k in range(3)]
-        lines += [middle[k : k + 1] for k in range(height)]
-        lines += [low[k : k + 1] for k in range(3)]
-        for k, line in enumerate(lines):
-            ext[k, at : at + 1, lanes : lanes + 4 * CH] = line
+        for k in range(3):
+            for line, first in ((top[height - 3 + k : height - 2 + k], k), (low[k : k + 1], 3 + height + k)):
+                ext[j, first * padded + at : first * padded + at + 1, :] = line
 
     lane = iota((padded, 4 * CH), 1)
     for k in range(height + 6):
-        before = pltpu.roll(ext[k, :, 4 * CH : 8 * CH], 1, 0)
-        after = pltpu.roll(ext[k, :, : 4 * CH], padded - 1, 0)
-        ext[k, :, 8 * CH :] = jnp.where(
+        before = pltpu.roll(ext[1, line_of(k), :], 1, 0)
+        after = pltpu.roll(ext[0, line_of(k), :], padded - 1, 0)
+        ext[2, line_of(k), :] = jnp.where(
             lane >= 3 * CH, before, jnp.where(lane < CH, after, 0.0)
         )
 
     lhs = jnp.concatenate(
         [
-            jnp.concatenate([ext[2 * k + e] for e in range(4)], axis=1)
+            jnp.concatenate([ext[j, line_of(2 * k + e), :] for e in range(4) for j in range(3)], axis=1)
             for k in range(half + 2)
         ],
         axis=0,
@@ -284,7 +336,10 @@
     for d in range(1, n):
         band_copy(d).start()
     bands_in[me] = pooled[pl.ds(me * stride, stride + 2)]
+    loads[4].wait()
     encoder_matrix(ew_ref, tenc)
+    loads[5].wait()
+    loads[6].wait()
     for d in range(1, n):
         band_arrival(d).wait_recv()
 
@@ -347,16 +402,23 @@
     blocks = valid_blocks.shape[1]
     half = height // 2
     stride = half // n
-    x = raw.reshape(height, groups, 8 * CH)
     vmem = pl.BlockSpec(memory_space=pltpu.VMEM)
     encoded = pl.pallas_call(
         functools.partial(kernel, sizes),
         out_shape=jax.ShapeDtypeStruct((n - 1, stride, groups, 4 * OUTC), BF16),
-        in_specs=[pl.BlockSpec(memory_space=pltpu.SMEM), pl.BlockSpec(memory_space=pl.ANY)] + [vmem] * 6,
+        in_specs=[pl.BlockSpec(memory_space=pltpu.HBM)] * 7,
         out_specs=vmem,
         scratch_shapes=[
-            pltpu.VMEM((height + 6, padded, 12 * CH), F32),
-            pltpu.VMEM((2, 3, groups, 8 * CH), BF16),
+            pltpu.SMEM((n,), jnp.int32),
+            pltpu.VMEM((height, lanes), BF16),
+            pltpu.VMEM((blocks, groups), jnp.int32),
+            pltpu.VMEM((CH, 9 * CH), BF16),
+            pltpu.VMEM((1, CH), F32),
+            pltpu.VMEM((OUTC, 27 * CH), BF16),
+            pltpu.VMEM((1, OUTC), F32),
+            pltpu.VMEM((3, (height + 6) * padded, 4 * CH), F32),
+            pltpu.VMEM((2, 3, padded, 8 * CH), BF16),
+            pltpu.VMEM((2, 3, padded, 8 * CH), BF16),
             pltpu.VMEM((9, height, 4 * CH), BF16),
             pltpu.VMEM((9, blocks, groups), jnp.int32),
             pltpu.VMEM((48 * CH, 8 * CH), BF16),
@@ -364,16 +426,17 @@
             pltpu.VMEM((half + 2, padded, 4 * CH), BF16),
             pltpu.VMEM((n, stride + 2, padded, 4 * CH), BF16),
             pltpu.VMEM((n, stride, padded, 12 * OUTC), F32),
+            pltpu.SemaphoreType.DMA((7,)),
             pltpu.SemaphoreType.DMA((9, 2)),
             pltpu.SemaphoreType.DMA((9, 2)),
             pltpu.SemaphoreType.DMA((n,)),
             pltpu.SemaphoreType.DMA((n,)),
         ],
         compiler_params=pltpu.CompilerParams(
-            collective_id=0, has_side_effects=True, vmem_limit_bytes=40 * 1024 * 1024
+            collective_id=0, has_side_effects=True, vmem_limit_bytes=64 * 1024 * 1024
         ),
     )(
-        owner_map, raw, x, valid_blocks[0], deblock_weight.T, deblock_bias[None], encoder_weight.T,
+        owner_map, raw, valid_blocks[0], deblock_weight.T, deblock_bias[None], encoder_weight.T,
         encoder_bias[None],
     )
     return encoded.reshape(n - 1, 1, stride, groups * 4 * OUTC)

time: 15.9 us -> 14.9 us (0.937)
  local copies, waits for them, and re-layouts: 2.55 us -> 1.41 us
  Pallas kernels: 13.1 us -> 13.3 us
    another operation x1 -> x0, local copies, waits for them, and re-layouts: 0.99 us -> none  [on_device(): x = raw.reshape(height, groups, 8 * CH)]
    unnamed x14 -> x0, local copies, waits for them, and re-layouts: 0.92 us -> none
    reshape x1, local copies, waits for them, and re-layouts: 0.64 us -> 1.41 us  [on_device(): return encoded.reshape(n - 1, 1, stride, groups * 4 * OUTC)]
    pallas_call x1, Pallas kernels: 13.1 us -> 13.3 us  [on_device(): pl.pallas_call(functools.partial(kernel, sizes), out_shape=jax.ShapeDtype...]
where the time goes in v2:
time: 14.9 us; the launch traced here: 14.7 us
  Pallas kernels  13.3 us (89%)
  local copies, waits for them, and re-layouts  1.41 us (9%)
    pallas_call x1, Pallas kernels, on_device(): pl.pallas_call(functools.partial(kernel, sizes), out_shape=jax.ShapeDtype...  13.3 us
    reshape x1, local copies, waits for them, and re-layouts, on_device(): return encoded.reshape(n - 1, 1, stride, groups * 4 * OUTC)  1.41 us

profile of v2, /device:TPU:0, one launch (start us, length us, event | category | flops | bytes accessed | tf_op | source)
XLA Modules:
  0.0 14.7 jit_solution(14736932781194727801)
XLA Ops:
  0.0 13.3 %shard_map.73 = bf16[3,1,18,256]{3,2,1,0:T(8,128)(2,1)} custom-call(s32[4]{0:T(128)} %owner_hbm.1, bf16[8,4608]{1,0:T(8,128)(2,1)} %bitcast.7, s32[1,18]{1,0:T(1,128)} %bitcast.9, bf16[32,288]{1,0:T(8,128)(2,1)} %bitcast.8, f32[1,32]{1,0:T(1,128)} %bitcast.10, bf16[64,864]{1,0:T(8,128)(2,1)} %bitcast.6, f32[1,64]{1,0:T(1,128)} %bitcast.11), custom_call_target="tpu_custom_call" | custom-call | tf_op jit(solution)/shard_map/pallas_call | solution.py:406
  13.3 1.4 %reshape.3 = bf16[3,1,1,4608]{3,0,2,1:T(4,128)(2,1)} reshape(bf16[3,1,18,256]{3,2,1,0:T(8,128)(2,1)} %shard_map.73) | data formatting | bytes 55296 | tf_op jit(solution)/shard_map/reshape | solution.py:442

commit v3 on v2

--- a/solution.py
+++ b/solution.py
@@ -122,6 +122,7 @@
     pooled,
     bands_in,
     product,
+    lines,
     load_sem,
     send_sem,
     recv_sem,
@@ -311,41 +312,43 @@
             part[:, 4 * CH :] + masks[which] * (part[:, : 4 * CH] + deblock_bias)
         ).astype(BF16)
 
-    def band_copy(d):
-        to = lax.rem(me + d, n)
+    def band_copy(to):
         return pltpu.make_async_remote_copy(
             src_ref=pooled.at[pl.ds(to * stride, stride + 2)],
             dst_ref=bands_in.at[me],
-            send_sem=band_send.at[d],
-            recv_sem=band_recv.at[d],
+            send_sem=band_send.at[to],
+            recv_sem=band_recv.at[me],
             device_id={"tm": to},
             device_id_type=MESH,
         )
 
-    def band_arrival(d):
-        source = lax.rem(me + n - d, n)
+    def band_arrival(source):
         return pltpu.make_async_remote_copy(
             src_ref=pooled.at[pl.ds(0, stride + 2)],
             dst_ref=bands_in.at[source],
-            send_sem=band_send.at[d],
-            recv_sem=band_recv.at[d],
+            send_sem=band_send.at[source],
+            recv_sem=band_recv.at[source],
             device_id={"tm": source},
             device_id_type=MESH,
         )
 
-    for d in range(1, n):
-        band_copy(d).start()
+    first, last = jnp.int32(0), jnp.int32(n - 1)
+    for _ in range(n - 1):
+        down = me - first > last - me
+        to = jnp.where(down, first, last)
+        band_copy(to).start()
+        first, last = jnp.where(down, first + 1, first), jnp.where(down, last, last - 1)
     bands_in[me] = pooled[pl.ds(me * stride, stride + 2)]
     loads[4].wait()
     encoder_matrix(ew_ref, tenc)
     loads[5].wait()
     loads[6].wait()
     for d in range(1, n):
-        band_arrival(d).wait_recv()
+        band_arrival(lax.rem(me + d, n)).wait_recv()
 
     rows = []
     for s in range(n):
-        lines = []
+        shifted = []
         for k in range(stride + 2):
             own = bands_in[s, k].astype(F32)
             side = jnp.where(
@@ -353,9 +356,9 @@
                 pltpu.roll(own, 1, 0),
                 jnp.where(lane < CH, pltpu.roll(own, padded - 1, 0), 0.0),
             )
-            lines.append(jnp.concatenate([own, side], axis=1))
+            shifted.append(jnp.concatenate([own, side], axis=1))
         for k in range(stride):
-            rows.append(jnp.concatenate(lines[k : k + 3], axis=1))
+            rows.append(jnp.concatenate(shifted[k : k + 3], axis=1))
     lhs = jnp.concatenate(rows, axis=0).astype(BF16)
     found = jnp.dot(lhs, tenc[...], preferred_element_type=F32)
     product[...] = found.reshape(product.shape)
@@ -378,7 +381,14 @@
             total = encoder_bias
             for lag in range(3):
                 total = total + product[slots[max(t - lag, 0)], k, :, lag * width : (lag + 1) * width]
-            out_ref[t - 1, k] = total[:groups].astype(BF16)
+            for j in range(2):
+                lines[j, line_of((t - 1) * stride + k), :] = total[:, j * 4 * CH : (j + 1) * 4 * CH]
+    for h in range(0, (n - 1) * stride, 8):
+        count = min(8, (n - 1) * stride - h)
+        for q in range(2 * groups):
+            out_ref[h : h + count, q * 4 * CH : (q + 1) * 4 * CH] = lines[
+                q % 2, pl.ds(h * padded + q // 2, count, stride=padded), :
+            ].astype(BF16)
 
     for dr, dc in DIRECTIONS:
 
@@ -388,7 +398,7 @@
                 copy.wait_send()
 
     for d in range(1, n):
-        band_copy(d).wait_send()
+        band_copy(lax.rem(me + d, n)).wait_send()
 
 
 def on_device(
@@ -403,9 +413,13 @@
     half = height // 2
     stride = half // n
     vmem = pl.BlockSpec(memory_space=pltpu.VMEM)
+    operands = (
+        owner_map, raw, valid_blocks[0], deblock_weight.T, deblock_bias[None], encoder_weight.T,
+        encoder_bias[None],
+    )
     encoded = pl.pallas_call(
         functools.partial(kernel, sizes),
-        out_shape=jax.ShapeDtypeStruct((n - 1, stride, groups, 4 * OUTC), BF16),
+        out_shape=jax.ShapeDtypeStruct(((n - 1) * stride, groups * 4 * OUTC), BF16),
         in_specs=[pl.BlockSpec(memory_space=pltpu.HBM)] * 7,
         out_specs=vmem,
         scratch_shapes=[
@@ -426,6 +440,7 @@
             pltpu.VMEM((half + 2, padded, 4 * CH), BF16),
             pltpu.VMEM((n, stride + 2, padded, 4 * CH), BF16),
             pltpu.VMEM((n, stride, padded, 12 * OUTC), F32),
+            pltpu.VMEM((2, (n - 1) * stride * padded, 4 * CH), F32),
             pltpu.SemaphoreType.DMA((7,)),
             pltpu.SemaphoreType.DMA((9, 2)),
             pltpu.SemaphoreType.DMA((9, 2)),
@@ -433,12 +448,9 @@
             pltpu.SemaphoreType.DMA((n,)),
         ],
         compiler_params=pltpu.CompilerParams(
-            collective_id=0, has_side_effects=True, vmem_limit_bytes=64 * 1024 * 1024
+            collective_id=0, has_side_effects=True, vmem_limit_bytes=40 * 1024 * 1024
         ),
-    )(
-        owner_map, raw, valid_blocks[0], deblock_weight.T, deblock_bias[None], encoder_weight.T,
-        encoder_bias[None],
-    )
+    )(*[pltpu.with_memory_space_constraint(operand, pltpu.HBM) for operand in operands])
     return encoded.reshape(n - 1, 1, stride, groups * 4 * OUTC)
 
 

time: 14.9 us -> 13.5 us (0.906)
  local copies, waits for them, and re-layouts: 1.41 us -> 0.62 us
  Pallas kernels: 13.3 us -> 12.8 us
    reshape x1 -> x0, local copies, waits for them, and re-layouts: 1.41 us -> none  [on_device(): return encoded.reshape(n - 1, 1, stride, groups * 4 * OUTC)]
    unnamed x0 -> x1, local copies, waits for them, and re-layouts: none -> 0.62 us
    pallas_call x1, Pallas kernels: 13.3 us -> 12.8 us  [on_device(): pl.pallas_call(functools.partial(kernel, sizes), out_shape=jax.ShapeDtype...]
where the time goes in v3:
time: 13.5 us; the launch traced here: 13.4 us
  Pallas kernels  12.8 us (95%)
  local copies, waits for them, and re-layouts  0.62 us (5%)
    pallas_call x1, Pallas kernels, on_device(): pl.pallas_call(functools.partial(kernel, sizes), out_shape=jax.ShapeDtype...  12.8 us
    unnamed x1, local copies, waits for them, and re-layouts  0.62 us

profile of v3, /device:TPU:0, one launch (start us, length us, event | category | flops | bytes accessed | tf_op | source)
XLA Modules:
  0.0 13.4 jit_solution(13580541583617173492)
XLA Ops:
  0.0 12.8 %shard_map.73 = bf16[3,4608]{1,0:T(4,128)(2,1)S(1)} custom-call(s32[4]{0:T(128)} %owner_hbm.1, bf16[8,4608]{1,0:T(8,128)(2,1)} %bitcast.9, s32[1,18]{1,0:T(1,128)} %bitcast.11, bf16[32,288]{1,0:T(8,128)(2,1)} %bitcast.10, f32[1,32]{1,0:T(1,128)} %bitcast.12, bf16[64,864]{1,0:T(8,128)(2,1)} %bitcast.8, f32[1,64]{1,0:T(1,128)} %bitcast.13), custom_call_target="tpu_custom_call" | custom-call | tf_op jit(solution)/shard_map/pallas_call | solution.py:420
  12.8 0.6 %copy.9 = bf16[3,1,1,4608]{3,0,2,1:T(4,128)(2,1)} copy(bf16[3,1,1,4608]{3,0,2,1:T(4,128)(2,1)S(1)} %bitcast.7) | data formatting | bytes 55296

commit v4 on v3

--- a/solution.py
+++ b/solution.py
@@ -113,14 +113,13 @@
     ew_ref,
     eb_ref,
     ext,
-    outgoing,
-    halo,
     edge,
     flags,
     tdeb,
     tenc,
     pooled,
     bands_in,
+    beside,
     product,
     lines,
     load_sem,
@@ -128,11 +127,13 @@
     recv_sem,
     band_send,
     band_recv,
+    beside_send,
+    beside_recv,
 ):
     n, nr, nc = sizes
     height, width = raw_ref.shape
     groups = width // (8 * CH)
-    padded = halo.shape[2]
+    padded = pooled.shape[1]
     half = height // 2
     stride = half // n
     me = lax.axis_index("tm")
@@ -156,9 +157,9 @@
     for load in loads:
         load.start()
 
-    halo[...] = jnp.zeros_like(halo)
     edge[...] = jnp.zeros_like(edge)
     flags[...] = jnp.zeros_like(flags)
+    beside[...] = jnp.zeros_like(beside)
 
     def exists(dr, dc):
         found = None
@@ -175,27 +176,25 @@
             to["row"] = r + dr
         if dc:
             to["col"] = c + dc
-        if dc:
-            lanes = pl.ds(0, 4 * CH) if dc < 0 else pl.ds(raw_ref.shape[1] - 4 * CH, 4 * CH)
-            src, dst = raw_ref.at[:, lanes], edge.at[there]
-        else:
-            src = outgoing.at[0 if dr < 0 else 1]
-            dst = halo.at[1 if dr < 0 else 0]
+        pairs = [(vb_hbm, flags.at[there])]
+        if not dr:
+            lanes = pl.ds(0 if dc < 0 else width - 4 * CH, 4 * CH)
+            pairs.append((raw_hbm.at[:, lanes], edge.at[(1 - dc) // 2]))
         return [
             pltpu.make_async_remote_copy(
                 src_ref=a, dst_ref=b, send_sem=send_sem.at[here, k], recv_sem=recv_sem.at[there, k],
                 device_id=to, device_id_type=MESH,
             )
-            for k, (a, b) in enumerate(((src, dst), (vb_ref, flags.at[there])))
+            for k, (a, b) in enumerate(pairs)
         ]
 
     barrier = pltpu.get_barrier_semaphore()
     for dr, dc in DIRECTIONS:
-        to = {}
+        if not dc:
+            continue
+        to = {"col": c + dc}
         if dr:
             to["row"] = r + dr
-        if dc:
-            to["col"] = c + dc
 
         @pl.when(exists(dr, dc))
         def _():
@@ -205,6 +204,26 @@
         pl.semaphore_signal(
             barrier, inc=1, device_id={"tm": lax.rem(me + d, n)}, device_id_type=MESH
         )
+    for dr in (-1, 1):
+
+        @pl.when(exists(dr, 0))
+        def _():
+            for t in range(n):
+                pl.semaphore_signal(
+                    barrier, inc=1, device_id={"tm": t, "row": r + dr}, device_id_type=MESH
+                )
+
+    tall = (r > 0).astype(jnp.int32) + (r < nr - 1).astype(jnp.int32) + 1
+    broad = (c > 0).astype(jnp.int32) + (c < nc - 1).astype(jnp.int32)
+    pl.semaphore_wait(barrier, tall * broad + tall * n - 1)
+
+    for dr, dc in sorted(DIRECTIONS, key=lambda item: item[0] != 0):
+
+        @pl.when(exists(dr, dc))
+        def _():
+            for copy in reversed(copies(dr, dc)):
+                copy.start()
+
     ext[...] = jnp.zeros_like(ext)
 
     def line_of(k):
@@ -213,30 +232,11 @@
     loads[0].wait()
     for h in range(0, height, 8):
         for q in range(2 * groups):
-            ext[q % 2, pl.ds((3 + h) * padded + q // 2, 8, stride=padded), :] = raw_ref[
+            ext[q % 2, pl.ds(h * padded + q // 2, 8, stride=padded), :] = raw_ref[
                 h : h + 8, q * 4 * CH : (q + 1) * 4 * CH
             ].astype(F32)
-    for side, dr in enumerate((-1, 1)):
-
-        @pl.when(exists(dr, 0))
-        def _():
-            for k in range(3):
-                line = line_of(3 + k if dr < 0 else height + k)
-                for j in range(2):
-                    outgoing[side, k, :, j * 4 * CH : (j + 1) * 4 * CH] = ext[j, line, :].astype(BF16)
 
     loads[1].wait()
-    tall = (r > 0).astype(jnp.int32) + (r < nr - 1).astype(jnp.int32) + 1
-    broad = (c > 0).astype(jnp.int32) + (c < nc - 1).astype(jnp.int32) + 1
-    pl.semaphore_wait(barrier, tall * broad - 1 + n - 1)
-
-    for dr, dc in DIRECTIONS:
-
-        @pl.when(exists(dr, dc))
-        def _():
-            for copy in copies(dr, dc):
-                copy.start()
-
     loads[2].wait()
     loads[3].wait()
     deblock_matrix(dw_ref, tdeb)
@@ -248,34 +248,29 @@
             for copy in copies(-dr, -dc):
                 copy.wait_recv()
 
-    for side, first in ((0, 0), (1, 3 + height)):
-        for k in range(3):
-            for j in range(2):
-                ext[j, line_of(first + k), :] = halo[
-                    side, k, :, j * 4 * CH : (j + 1) * 4 * CH
-                ].astype(F32)
-    for dc, at, j in ((-1, padded - 1, 1), (1, groups, 0)):
+    for side, at, j in ((0, padded - 1, 1), (1, groups, 0)):
         for h in range(0, height, 8):
-            ext[j, pl.ds((3 + h) * padded + at, 8, stride=padded), :] = edge[
-                place(0, dc), h : h + 8
-            ].astype(F32)
-        top = edge[place(-1, dc)].astype(F32)
-        low = edge[place(1, dc)].astype(F32)
-        for k in range(3):
-            for line, first in ((top[height - 3 + k : height - 2 + k], k), (low[k : k + 1], 3 + height + k)):
-                ext[j, first * padded + at : first * padded + at + 1, :] = line
+            ext[j, pl.ds(h * padded + at, 8, stride=padded), :] = edge[side, h : h + 8].astype(F32)
 
     lane = iota((padded, 4 * CH), 1)
-    for k in range(height + 6):
+    for k in range(height):
         before = pltpu.roll(ext[1, line_of(k), :], 1, 0)
         after = pltpu.roll(ext[0, line_of(k), :], padded - 1, 0)
         ext[2, line_of(k), :] = jnp.where(
             lane >= 3 * CH, before, jnp.where(lane < CH, after, 0.0)
         )
 
+    nothing = jnp.zeros((padded, 4 * CH), F32)
     lhs = jnp.concatenate(
         [
-            jnp.concatenate([ext[j, line_of(2 * k + e), :] for e in range(4) for j in range(3)], axis=1)
+            jnp.concatenate(
+                [
+                    ext[j, line_of(2 * k + e - 3), :] if 0 <= 2 * k + e - 3 < height else nothing
+                    for e in range(4)
+                    for j in range(3)
+                ],
+                axis=1,
+            )
             for k in range(half + 2)
         ],
         axis=0,
@@ -308,9 +303,10 @@
     for k in range(half + 2):
         part = conv[k * padded : (k + 1) * padded]
         which = 0 if k == 0 else blocks + 1 if k == half + 1 else 1 + (k - 1) // per
-        pooled[k] = (
-            part[:, 4 * CH :] + masks[which] * (part[:, : 4 * CH] + deblock_bias)
-        ).astype(BF16)
+        term = part[:, : 4 * CH]
+        if 1 <= k <= half:
+            term = term + deblock_bias
+        pooled[k] = (part[:, 4 * CH :] + masks[which] * term).astype(BF16)
 
     def band_copy(to):
         return pltpu.make_async_remote_copy(
@@ -331,6 +327,31 @@
             device_id={"tm": source},
             device_id_type=MESH,
         )
+
+    spreads = []
+    for side, dr in enumerate((1, -1)):
+        for gap in range(2 if stride == 1 else 1):
+            band = gap if dr > 0 else n - 1 - gap
+            source = half + gap if dr > 0 else 0
+            target = 0 if dr > 0 else stride + gap
+            spreads.append((side, dr, gap, band, pl.ds(source, 2 - gap), pl.ds(target, 2 - gap)))
+
+    def beside_copy(item, frame):
+        side, dr, gap, band, source, target = item
+        return pltpu.make_async_remote_copy(
+            src_ref=pooled.at[source],
+            dst_ref=beside.at[side, frame, target],
+            send_sem=beside_send.at[side, gap],
+            recv_sem=beside_recv.at[side, frame],
+            device_id={"tm": band, "row": r + dr},
+            device_id_type=MESH,
+        )
+
+    for item in spreads:
+
+        @pl.when(exists(item[1], 0))
+        def _():
+            beside_copy(item, me).start()
 
     first, last = jnp.int32(0), jnp.int32(n - 1)
     for _ in range(n - 1):
@@ -345,12 +366,18 @@
     loads[6].wait()
     for d in range(1, n):
         band_arrival(lax.rem(me + d, n)).wait_recv()
+    for item in spreads:
+
+        @pl.when(jnp.logical_and(exists(-item[1], 0), me == item[3]))
+        def _():
+            for frame in range(n):
+                beside_copy(item, frame).wait_recv()
 
     rows = []
     for s in range(n):
         shifted = []
         for k in range(stride + 2):
-            own = bands_in[s, k].astype(F32)
+            own = bands_in[s, k].astype(F32) + beside[0, s, k].astype(F32) + beside[1, s, k].astype(F32)
             side = jnp.where(
                 lane >= 3 * CH,
                 pltpu.roll(own, 1, 0),
@@ -399,6 +426,12 @@
 
     for d in range(1, n):
         band_copy(lax.rem(me + d, n)).wait_send()
+
+    for item in spreads:
+
+        @pl.when(exists(item[1], 0))
+        def _():
+            beside_copy(item, me).wait_send()
 
 
 def on_device(
@@ -430,15 +463,14 @@
             pltpu.VMEM((1, CH), F32),
             pltpu.VMEM((OUTC, 27 * CH), BF16),
             pltpu.VMEM((1, OUTC), F32),
-            pltpu.VMEM((3, (height + 6) * padded, 4 * CH), F32),
-            pltpu.VMEM((2, 3, padded, 8 * CH), BF16),
-            pltpu.VMEM((2, 3, padded, 8 * CH), BF16),
-            pltpu.VMEM((9, height, 4 * CH), BF16),
+            pltpu.VMEM((3, height * padded, 4 * CH), F32),
+            pltpu.VMEM((2, height, 4 * CH), BF16),
             pltpu.VMEM((9, blocks, groups), jnp.int32),
             pltpu.VMEM((48 * CH, 8 * CH), BF16),
             pltpu.VMEM((24 * CH, 12 * OUTC), BF16),
             pltpu.VMEM((half + 2, padded, 4 * CH), BF16),
             pltpu.VMEM((n, stride + 2, padded, 4 * CH), BF16),
+            pltpu.VMEM((2, n, stride + 2, padded, 4 * CH), BF16),
             pltpu.VMEM((n, stride, padded, 12 * OUTC), F32),
             pltpu.VMEM((2, (n - 1) * stride * padded, 4 * CH), F32),
             pltpu.SemaphoreType.DMA((7,)),
@@ -446,6 +478,8 @@
             pltpu.SemaphoreType.DMA((9, 2)),
             pltpu.SemaphoreType.DMA((n,)),
             pltpu.SemaphoreType.DMA((n,)),
+            pltpu.SemaphoreType.DMA((2, 2)),
+            pltpu.SemaphoreType.DMA((2, n)),
         ],
         compiler_params=pltpu.CompilerParams(
             collective_id=0, has_side_effects=True, vmem_limit_bytes=40 * 1024 * 1024

time: 13.5 us -> 13.9 us (1.030)
  Pallas kernels: 12.8 us -> 13.1 us
    pallas_call x1, Pallas kernels: 12.8 us -> 13.1 us  [on_device(): pl.pallas_call(functools.partial(kernel, sizes), out_shape=jax.ShapeDtype...]
where the time goes in v4:
time: 13.9 us; the launch traced here: 13.7 us
  Pallas kernels  13.1 us (94%)
  local copies, waits for them, and re-layouts  0.62 us (4%)
    pallas_call x1, Pallas kernels, on_device(): pl.pallas_call(functools.partial(kernel, sizes), out_shape=jax.ShapeDtype...  13.1 us
    unnamed x1, local copies, waits for them, and re-layouts  0.62 us

profile of v4, /device:TPU:0, one launch (start us, length us, event | category | flops | bytes accessed | tf_op | source)
XLA Modules:
  0.0 13.7 jit_solution(14728728483065826733)
XLA Ops:
  0.0 13.1 %shard_map.73 = bf16[3,4608]{1,0:T(4,128)(2,1)S(1)} custom-call(s32[4]{0:T(128)} %owner_hbm.1, bf16[8,4608]{1,0:T(8,128)(2,1)} %bitcast.9, s32[1,18]{1,0:T(1,128)} %bitcast.11, bf16[32,288]{1,0:T(8,128)(2,1)} %bitcast.10, f32[1,32]{1,0:T(1,128)} %bitcast.12, bf16[64,864]{1,0:T(8,128)(2,1)} %bitcast.8, f32[1,64]{1,0:T(1,128)} %bitcast.13), custom_call_target="tpu_custom_call" | custom-call | tf_op jit(solution)/shard_map/pallas_call | solution.py:453
  13.1 0.6 %copy.9 = bf16[3,1,1,4608]{3,0,2,1:T(4,128)(2,1)} copy(bf16[3,1,1,4608]{3,0,2,1:T(4,128)(2,1)S(1)} %bitcast.7) | data formatting | bytes 55296

commit v5 on v3

--- a/solution.py
+++ b/solution.py
@@ -237,6 +237,17 @@
             for copy in copies(dr, dc):
                 copy.start()
 
+    lanes_of = iota((padded, 4 * CH), 1)
+
+    def beside(k):
+        before = pltpu.roll(ext[1, line_of(k), :], 1, 0)
+        after = pltpu.roll(ext[0, line_of(k), :], padded - 1, 0)
+        ext[2, line_of(k), :] = jnp.where(
+            lanes_of >= 3 * CH, before, jnp.where(lanes_of < CH, after, 0.0)
+        )
+
+    for k in range(3, 3 + height):
+        beside(k)
     loads[2].wait()
     loads[3].wait()
     deblock_matrix(dw_ref, tdeb)
@@ -265,13 +276,15 @@
             for line, first in ((top[height - 3 + k : height - 2 + k], k), (low[k : k + 1], 3 + height + k)):
                 ext[j, first * padded + at : first * padded + at + 1, :] = line
 
-    lane = iota((padded, 4 * CH), 1)
-    for k in range(height + 6):
-        before = pltpu.roll(ext[1, line_of(k), :], 1, 0)
-        after = pltpu.roll(ext[0, line_of(k), :], padded - 1, 0)
-        ext[2, line_of(k), :] = jnp.where(
-            lane >= 3 * CH, before, jnp.where(lane < CH, after, 0.0)
-        )
+    for k in (0, 1, 2, height + 3, height + 4, height + 5):
+        beside(k)
+    lane = iota((8, 4 * CH), 1)
+    for h in range(0, height, 8):
+        for side, at, j in ((0, 0, padded - 1), (1, groups - 1, groups)):
+            spot = pl.ds((3 + h) * padded + at, 8, stride=padded)
+            chosen = lane >= 3 * CH if side == 0 else lane < CH
+            came = edge[place(0, -1 if side == 0 else 1), h : h + 8].astype(F32)
+            ext[2, spot, :] = jnp.where(chosen, came, ext[2, spot, :])
 
     lhs = jnp.concatenate(
         [
@@ -333,36 +346,16 @@
         )
 
     first, last = jnp.int32(0), jnp.int32(n - 1)
+    order = []
     for _ in range(n - 1):
         down = me - first > last - me
         to = jnp.where(down, first, last)
         band_copy(to).start()
+        order.append(to)
         first, last = jnp.where(down, first + 1, first), jnp.where(down, last, last - 1)
-    bands_in[me] = pooled[pl.ds(me * stride, stride + 2)]
-    loads[4].wait()
+    for load in loads[4:]:
+        load.wait()
     encoder_matrix(ew_ref, tenc)
-    loads[5].wait()
-    loads[6].wait()
-    for d in range(1, n):
-        band_arrival(lax.rem(me + d, n)).wait_recv()
-
-    rows = []
-    for s in range(n):
-        shifted = []
-        for k in range(stride + 2):
-            own = bands_in[s, k].astype(F32)
-            side = jnp.where(
-                lane >= 3 * CH,
-                pltpu.roll(own, 1, 0),
-                jnp.where(lane < CH, pltpu.roll(own, padded - 1, 0), 0.0),
-            )
-            shifted.append(jnp.concatenate([own, side], axis=1))
-        for k in range(stride):
-            rows.append(jnp.concatenate(shifted[k : k + 3], axis=1))
-    lhs = jnp.concatenate(rows, axis=0).astype(BF16)
-    found = jnp.dot(lhs, tenc[...], preferred_element_type=F32)
-    product[...] = found.reshape(product.shape)
-
     slots = []
     for t in range(n):
         if n <= 8:
@@ -374,6 +367,27 @@
                 0, n, lambda s, held: jnp.where(owner_ref[s] == t, s, held), jnp.int32(0)
             )
         slots.append(slot)
+
+    def encode(frame, lines_in):
+        shifted = []
+        for own in lines_in:
+            side = jnp.where(
+                lanes_of >= 3 * CH,
+                pltpu.roll(own, 1, 0),
+                jnp.where(lanes_of < CH, pltpu.roll(own, padded - 1, 0), 0.0),
+            )
+            shifted.append(jnp.concatenate([own, side], axis=1))
+        rows = [jnp.concatenate(shifted[k : k + 3], axis=1) for k in range(stride)]
+        found = jnp.dot(
+            jnp.concatenate(rows, axis=0).astype(BF16), tenc[...], preferred_element_type=F32
+        )
+        product[frame] = found.reshape(stride, padded, 12 * OUTC)
+
+    encode(me, [pooled[me * stride + k].astype(F32) for k in range(stride + 2)])
+    for source in reversed(order):
+        band_arrival(source).wait_recv()
+        encode(source, [bands_in[source, k].astype(F32) for k in range(stride + 2)])
+
     width = 4 * OUTC
     encoder_bias = jnp.concatenate([eb_ref[...]] * 4, axis=1)
     for t in range(1, n):

time: 13.5 us -> 14 us (1.037)
  Pallas kernels: 12.8 us -> 13.2 us
    pallas_call x1, Pallas kernels: 12.8 us -> 13.2 us  [on_device(): pl.pallas_call(functools.partial(kernel, sizes), out_shape=jax.ShapeDtype...]
where the time goes in v5:
time: 14 us; the launch traced here: 13.9 us
  Pallas kernels  13.2 us (94%)
  local copies, waits for them, and re-layouts  0.62 us (4%)
    pallas_call x1, Pallas kernels, on_device(): pl.pallas_call(functools.partial(kernel, sizes), out_shape=jax.ShapeDtype...  13.2 us
    unnamed x1, local copies, waits for them, and re-layouts  0.62 us

profile of v5, /device:TPU:0, one launch (start us, length us, event | category | flops | bytes accessed | tf_op | source)
XLA Modules:
  0.0 13.9 jit_solution(8908164751324663455)
XLA Ops:
  0.0 13.2 %shard_map.73 = bf16[3,4608]{1,0:T(4,128)(2,1)S(1)} custom-call(s32[4]{0:T(128)} %owner_hbm.1, bf16[8,4608]{1,0:T(8,128)(2,1)} %bitcast.9, s32[1,18]{1,0:T(1,128)} %bitcast.11, bf16[32,288]{1,0:T(8,128)(2,1)} %bitcast.10, f32[1,32]{1,0:T(1,128)} %bitcast.12, bf16[64,864]{1,0:T(8,128)(2,1)} %bitcast.8, f32[1,64]{1,0:T(1,128)} %bitcast.13), custom_call_target="tpu_custom_call" | custom-call | tf_op jit(solution)/shard_map/pallas_call | solution.py:434
  13.2 0.6 %copy.9 = bf16[3,1,1,4608]{3,0,2,1:T(4,128)(2,1)} copy(bf16[3,1,1,4608]{3,0,2,1:T(4,128)(2,1)S(1)} %bitcast.7) | data formatting | bytes 55296

commit v6 on v5

--- a/solution.py
+++ b/solution.py
@@ -30,7 +30,9 @@
 
 
 def deblock_matrix(dw_ref, t_ref):
-    spread = (iota((CH, 4 * CH), 1) % CH == iota((CH, 4 * CH), 0)).astype(BF16)
+    block = iota((CH, 4 * CH), 1) // CH
+    same = iota((CH, 4 * CH), 1) - block * CH == iota((CH, 4 * CH), 0)
+    spread = same.astype(BF16)
     tiled = spread_taps(dw_ref[...], spread)
     taps = [[tiled[(3 * a + b) * CH : (3 * a + b + 1) * CH] for b in range(3)] for a in range(3)]
     wide = [
@@ -41,10 +43,9 @@
         [0.25 * sum(wide[a][d] for a in (e - 1, e) if 0 <= a < 3) for d in range(4)]
         for e in range(4)
     ]
-    block = iota((CH, 4 * CH), 1) // CH
     zero = jnp.zeros((CH, 4 * CH), F32)
-    rows, cols = iota((8 * CH, 4 * CH), 0), iota((8 * CH, 4 * CH), 1)
-    mean = jnp.where((rows // (2 * CH) == cols // CH) & (rows % CH == cols % CH), 0.25, 0.0).astype(BF16)
+    quarter = jnp.where(same, 0.25, 0.0)
+    means = [jnp.where(block == o, quarter, zero).astype(BF16) for o in range(4)]
     nothing = jnp.zeros((8 * CH, 4 * CH), BF16)
     for e in range(4):
         base = e * 12 * CH
@@ -62,37 +63,46 @@
         put(8, 8)
         put(11, -1)
         t_ref[base + 9 * CH : base + 11 * CH, : 4 * CH] = nothing[: 2 * CH]
-        t_ref[base : base + 8 * CH, 4 * CH :] = mean if e in (1, 2) else nothing
+        for pixel in range(8):
+            t_ref[base + pixel * CH : base + (pixel + 1) * CH, 4 * CH :] = (
+                means[pixel // 2] if e in (1, 2) else nothing[:CH]
+            )
         t_ref[base + 8 * CH : base + 12 * CH, 4 * CH :] = nothing[: 4 * CH]
 
 
 def encoder_matrix(ew_ref, t_ref):
-    width = 4 * OUTC
-    spread = (iota((OUTC, width), 1) % OUTC == iota((OUTC, width), 0)).astype(BF16)
-    block = iota((CH, width), 1) // OUTC
-    zero = jnp.zeros((CH, width), F32)
-    nothing = jnp.zeros((2 * CH, width), BF16)
-    everything = spread_taps(ew_ref[...], spread)
+    pair = 2 * OUTC
+    rows, cols = iota((OUTC, 2 * pair), 0), iota((OUTC, 2 * pair), 1)
+    spread = ((cols == rows) | (cols == rows + pair + OUTC)).astype(BF16)
+    everything = spread_taps(ew_ref[...], spread).astype(BF16)
+    nothing = jnp.zeros((2 * CH, 2 * pair), BF16)
     for lag in range(3):
-        tiled = everything[lag * 9 * CH : (lag + 1) * 9 * CH]
         for dy in range(3):
             base = dy * 8 * CH
-            left = lag * width
+            left = lag * 2 * pair
+            first = (lag * 9 + dy * 3) * CH
 
             def put(at, pixel):
-                total = zero
-                for o in range(4):
-                    d = pixel - o + 1
-                    if 0 <= d < 3:
-                        tap = tiled[(3 * dy + d) * CH : (3 * dy + d + 1) * CH]
-                        total = jnp.where(block == o, tap, total)
-                t_ref[base + at * CH : base + (at + 1) * CH, left : left + width] = total.astype(BF16)
+                for side in range(2):
+                    total = None
+                    for o in (2 * side, 2 * side + 1):
+                        d = pixel - o + 1
+                        if 0 <= d < 3:
+                            tap = everything[
+                                first + d * CH : first + (d + 1) * CH, (o % 2) * pair : (o % 2 + 1) * pair
+                            ]
+                            total = tap if total is None else total + tap
+                    if total is None:
+                        total = nothing[:CH, :pair]
+                    t_ref[
+                        base + at * CH : base + (at + 1) * CH, left + side * pair : left + (side + 1) * pair
+                    ] = total
 
             for pixel in range(4):
                 put(pixel, pixel)
             put(4, 4)
             put(7, -1)
-            t_ref[base + 5 * CH : base + 7 * CH, left : left + width] = nothing
+            t_ref[base + 5 * CH : base + 7 * CH, left : left + 2 * pair] = nothing
 
 
 def kernel(
@@ -251,6 +261,9 @@
     loads[2].wait()
     loads[3].wait()
     deblock_matrix(dw_ref, tdeb)
+    for load in loads[4:]:
+        load.wait()
+    encoder_matrix(ew_ref, tenc)
 
     for dr, dc in DIRECTIONS:
 
@@ -353,9 +366,6 @@
         band_copy(to).start()
         order.append(to)
         first, last = jnp.where(down, first + 1, first), jnp.where(down, last, last - 1)
-    for load in loads[4:]:
-        load.wait()
-    encoder_matrix(ew_ref, tenc)
     slots = []
     for t in range(n):
         if n <= 8:
@@ -368,25 +378,28 @@
             )
         slots.append(slot)
 
-    def encode(frame, lines_in):
-        shifted = []
-        for own in lines_in:
-            side = jnp.where(
-                lanes_of >= 3 * CH,
-                pltpu.roll(own, 1, 0),
-                jnp.where(lanes_of < CH, pltpu.roll(own, padded - 1, 0), 0.0),
-            )
-            shifted.append(jnp.concatenate([own, side], axis=1))
-        rows = [jnp.concatenate(shifted[k : k + 3], axis=1) for k in range(stride)]
+    def encode(frames, lines_in):
+        rows = []
+        for lines_of_frame in lines_in:
+            shifted = []
+            for own in lines_of_frame:
+                side = jnp.where(
+                    lanes_of >= 3 * CH,
+                    pltpu.roll(own, 1, 0),
+                    jnp.where(lanes_of < CH, pltpu.roll(own, padded - 1, 0), 0.0),
+                )
+                shifted.append(jnp.concatenate([own, side], axis=1))
+            rows += [jnp.concatenate(shifted[k : k + 3], axis=1) for k in range(stride)]
         found = jnp.dot(
             jnp.concatenate(rows, axis=0).astype(BF16), tenc[...], preferred_element_type=F32
-        )
-        product[frame] = found.reshape(stride, padded, 12 * OUTC)
-
-    encode(me, [pooled[me * stride + k].astype(F32) for k in range(stride + 2)])
-    for source in reversed(order):
+        ).reshape(len(frames), stride, padded, 12 * OUTC)
+        for k, frame in enumerate(frames):
+            product[frame] = found[k]
+
+    encode([me], [[pooled[me * stride + k].astype(F32) for k in range(stride + 2)]])
+    for source in order:
         band_arrival(source).wait_recv()
-        encode(source, [bands_in[source, k].astype(F32) for k in range(stride + 2)])
+    encode(order, [[bands_in[s, k].astype(F32) for k in range(stride + 2)] for s in order])
 
     width = 4 * OUTC
     encoder_bias = jnp.concatenate([eb_ref[...]] * 4, axis=1)

time: 14 us -> 13.6 us (0.971)
  Pallas kernels: 13.2 us -> 12.8 us
    pallas_call x1, Pallas kernels: 13.2 us -> 12.8 us  [on_device(): pl.pallas_call(functools.partial(kernel, sizes), out_shape=jax.ShapeDtype...]
where the time goes in v6:
time: 13.6 us; the launch traced here: 13.4 us
  Pallas kernels  12.8 us (94%)
  local copies, waits for them, and re-layouts  0.62 us (5%)
    pallas_call x1, Pallas kernels, on_device(): pl.pallas_call(functools.partial(kernel, sizes), out_shape=jax.ShapeDtype...  12.8 us
    unnamed x1, local copies, waits for them, and re-layouts  0.62 us

profile of v6, /device:TPU:0, one launch (start us, length us, event | category | flops | bytes accessed | tf_op | source)
XLA Modules:
  0.0 13.4 jit_solution(14630271545503428346)
XLA Ops:
  0.0 12.8 %shard_map.73 = bf16[3,4608]{1,0:T(4,128)(2,1)S(1)} custom-call(s32[4]{0:T(128)} %owner_hbm.1, bf16[8,4608]{1,0:T(8,128)(2,1)} %bitcast.9, s32[1,18]{1,0:T(1,128)} %bitcast.11, bf16[32,288]{1,0:T(8,128)(2,1)} %bitcast.10, f32[1,32]{1,0:T(1,128)} %bitcast.12, bf16[64,864]{1,0:T(8,128)(2,1)} %bitcast.8, f32[1,64]{1,0:T(1,128)} %bitcast.13), custom_call_target="tpu_custom_call" | custom-call | tf_op jit(solution)/shard_map/pallas_call | solution.py:447
  12.8 0.6 %copy.9 = bf16[3,1,1,4608]{3,0,2,1:T(4,128)(2,1)} copy(bf16[3,1,1,4608]{3,0,2,1:T(4,128)(2,1)S(1)} %bitcast.7) | data formatting | bytes 55296

commit v7 on v6

--- a/solution.py
+++ b/solution.py
@@ -235,7 +235,13 @@
                 for j in range(2):
                     outgoing[side, k, :, j * 4 * CH : (j + 1) * 4 * CH] = ext[j, line, :].astype(BF16)
 
-    loads[1].wait()
+    for load in loads[1:]:
+        load.wait()
+
+    @pl.when(me < n // 2)
+    def _():
+        encoder_matrix(ew_ref, tenc)
+
     tall = (r > 0).astype(jnp.int32) + (r < nr - 1).astype(jnp.int32) + 1
     broad = (c > 0).astype(jnp.int32) + (c < nc - 1).astype(jnp.int32) + 1
     pl.semaphore_wait(barrier, tall * broad - 1 + n - 1)
@@ -258,12 +264,7 @@
 
     for k in range(3, 3 + height):
         beside(k)
-    loads[2].wait()
-    loads[3].wait()
     deblock_matrix(dw_ref, tdeb)
-    for load in loads[4:]:
-        load.wait()
-    encoder_matrix(ew_ref, tenc)
 
     for dr, dc in DIRECTIONS:
 
@@ -358,14 +359,14 @@
             device_id_type=MESH,
         )
 
-    first, last = jnp.int32(0), jnp.int32(n - 1)
-    order = []
-    for _ in range(n - 1):
-        down = me - first > last - me
-        to = jnp.where(down, first, last)
+    order = [jnp.where(me > k, k, k + 1) for k in range(n - 1)]
+    for to in order:
         band_copy(to).start()
-        order.append(to)
-        first, last = jnp.where(down, first + 1, first), jnp.where(down, last, last - 1)
+
+    @pl.when(me >= n // 2)
+    def _():
+        encoder_matrix(ew_ref, tenc)
+
     slots = []
     for t in range(n):
         if n <= 8:

time: 13.6 us -> 13.5 us (level)
  no operation moved by 1% of the time
where the time goes in v7:
time: 13.5 us; the launch traced here: 13.4 us
  Pallas kernels  12.8 us (95%)
  local copies, waits for them, and re-layouts  0.62 us (5%)
    pallas_call x1, Pallas kernels, on_device(): pl.pallas_call(functools.partial(kernel, sizes), out_shape=jax.ShapeDtype...  12.8 us
    unnamed x1, local copies, waits for them, and re-layouts  0.62 us

profile of v7, /device:TPU:0, one launch (start us, length us, event | category | flops | bytes accessed | tf_op | source)
XLA Modules:
  0.0 13.4 jit_solution(13484471214855481131)
XLA Ops:
  0.0 12.8 %shard_map.73 = bf16[3,4608]{1,0:T(4,128)(2,1)S(1)} custom-call(s32[4]{0:T(128)} %owner_hbm.1, bf16[8,4608]{1,0:T(8,128)(2,1)} %bitcast.9, s32[1,18]{1,0:T(1,128)} %bitcast.11, bf16[32,288]{1,0:T(8,128)(2,1)} %bitcast.10, f32[1,32]{1,0:T(1,128)} %bitcast.12, bf16[64,864]{1,0:T(8,128)(2,1)} %bitcast.8, f32[1,64]{1,0:T(1,128)} %bitcast.13), custom_call_target="tpu_custom_call" | custom-call | tf_op jit(solution)/shard_map/pallas_call | solution.py:448
  12.8 0.6 %copy.9 = bf16[3,1,1,4608]{3,0,2,1:T(4,128)(2,1)} copy(bf16[3,1,1,4608]{3,0,2,1:T(4,128)(2,1)S(1)} %bitcast.7) | data formatting | bytes 55296

commit v8 on v7

--- a/solution.py
+++ b/solution.py
@@ -142,7 +142,7 @@
     n, nr, nc = sizes
     height, width = raw_ref.shape
     groups = width // (8 * CH)
-    padded = halo.shape[2]
+    padded = pooled.shape[1]
     half = height // 2
     stride = half // n
     me = lax.axis_index("tm")
@@ -233,7 +233,7 @@
             for k in range(3):
                 line = line_of(3 + k if dr < 0 else height + k)
                 for j in range(2):
-                    outgoing[side, k, :, j * 4 * CH : (j + 1) * 4 * CH] = ext[j, line, :].astype(BF16)
+                    outgoing[side, k, :, j * 4 * CH : (j + 1) * 4 * CH] = ext[j, line, :][:groups].astype(BF16)
 
     for load in loads[1:]:
         load.wait()
@@ -246,12 +246,12 @@
     broad = (c > 0).astype(jnp.int32) + (c < nc - 1).astype(jnp.int32) + 1
     pl.semaphore_wait(barrier, tall * broad - 1 + n - 1)
 
-    for dr, dc in DIRECTIONS:
-
-        @pl.when(exists(dr, dc))
-        def _():
-            for copy in copies(dr, dc):
-                copy.start()
+    for k in range(2):
+        for dr, dc in sorted(DIRECTIONS, key=lambda item: item[1] != 0):
+
+            @pl.when(exists(dr, dc))
+            def _():
+                copies(dr, dc)[k].start()
 
     lanes_of = iota((padded, 4 * CH), 1)
 
@@ -276,7 +276,7 @@
     for side, first in ((0, 0), (1, 3 + height)):
         for k in range(3):
             for j in range(2):
-                ext[j, line_of(first + k), :] = halo[
+                ext[j, pl.ds((first + k) * padded, groups), :] = halo[
                     side, k, :, j * 4 * CH : (j + 1) * 4 * CH
                 ].astype(F32)
     for dc, at, j in ((-1, padded - 1, 1), (1, groups, 0)):
@@ -459,8 +459,8 @@
             pltpu.VMEM((OUTC, 27 * CH), BF16),
             pltpu.VMEM((1, OUTC), F32),
             pltpu.VMEM((3, (height + 6) * padded, 4 * CH), F32),
-            pltpu.VMEM((2, 3, padded, 8 * CH), BF16),
-            pltpu.VMEM((2, 3, padded, 8 * CH), BF16),
+            pltpu.VMEM((2, 3, groups, 8 * CH), BF16),
+            pltpu.VMEM((2, 3, groups, 8 * CH), BF16),
             pltpu.VMEM((9, height, 4 * CH), BF16),
             pltpu.VMEM((9, blocks, groups), jnp.int32),
             pltpu.VMEM((48 * CH, 8 * CH), BF16),

time: 13.5 us -> 13.5 us (level)
  no operation moved by 1% of the time
where the time goes in v8:
time: 13.5 us; the launch traced here: 13.4 us
  Pallas kernels  12.7 us (94%)
  local copies, waits for them, and re-layouts  0.62 us (5%)
    pallas_call x1, Pallas kernels, on_device(): pl.pallas_call(functools.partial(kernel, sizes), out_shape=jax.ShapeDtype...  12.7 us
    unnamed x1, local copies, waits for them, and re-layouts  0.62 us

profile of v8, /device:TPU:0, one launch (start us, length us, event | category | flops | bytes accessed | tf_op | source)
XLA Modules:
  0.0 13.4 jit_solution(17630274452890230181)
XLA Ops:
  0.0 12.7 %shard_map.73 = bf16[3,4608]{1,0:T(4,128)(2,1)S(1)} custom-call(s32[4]{0:T(128)} %owner_hbm.1, bf16[8,4608]{1,0:T(8,128)(2,1)} %bitcast.9, s32[1,18]{1,0:T(1,128)} %bitcast.11, bf16[32,288]{1,0:T(8,128)(2,1)} %bitcast.10, f32[1,32]{1,0:T(1,128)} %bitcast.12, bf16[64,864]{1,0:T(8,128)(2,1)} %bitcast.8, f32[1,64]{1,0:T(1,128)} %bitcast.13), custom_call_target="tpu_custom_call" | custom-call | tf_op jit(solution)/shard_map/pallas_call | solution.py:448
  12.8 0.6 %copy.9 = bf16[3,1,1,4608]{3,0,2,1:T(4,128)(2,1)} copy(bf16[3,1,1,4608]{3,0,2,1:T(4,128)(2,1)S(1)} %bitcast.7) | data formatting | bytes 55296

commit v9 on v8

--- a/solution.py
+++ b/solution.py
@@ -398,9 +398,11 @@
             product[frame] = found[k]
 
     encode([me], [[pooled[me * stride + k].astype(F32) for k in range(stride + 2)]])
-    for source in order:
-        band_arrival(source).wait_recv()
-    encode(order, [[bands_in[s, k].astype(F32) for k in range(stride + 2)] for s in order])
+    for batch in (order[:-1], order[-1:]):
+        for source in batch:
+            band_arrival(source).wait_recv()
+        if batch:
+            encode(batch, [[bands_in[s, k].astype(F32) for k in range(stride + 2)] for s in batch])
 
     width = 4 * OUTC
     encoder_bias = jnp.concatenate([eb_ref[...]] * 4, axis=1)

time: 13.5 us -> 13.9 us (1.030)
  Pallas kernels: 12.7 us -> 13.1 us
    pallas_call x1, Pallas kernels: 12.7 us -> 13.1 us  [on_device(): pl.pallas_call(functools.partial(kernel, sizes), out_shape=jax.ShapeDtype...]
where the time goes in v9:
time: 13.9 us; the launch traced here: 13.7 us
  Pallas kernels  13.1 us (94%)
  local copies, waits for them, and re-layouts  0.62 us (4%)
    pallas_call x1, Pallas kernels, on_device(): pl.pallas_call(functools.partial(kernel, sizes), out_shape=jax.ShapeDtype...  13.1 us
    unnamed x1, local copies, waits for them, and re-layouts  0.62 us

profile of v9, /device:TPU:0, one launch (start us, length us, event | category | flops | bytes accessed | tf_op | source)
XLA Modules:
  0.0 13.7 jit_solution(17983621186128368613)
XLA Ops:
  0.0 13.1 %shard_map.73 = bf16[3,4608]{1,0:T(4,128)(2,1)S(1)} custom-call(s32[4]{0:T(128)} %owner_hbm.1, bf16[8,4608]{1,0:T(8,128)(2,1)} %bitcast.9, s32[1,18]{1,0:T(1,128)} %bitcast.11, bf16[32,288]{1,0:T(8,128)(2,1)} %bitcast.10, f32[1,32]{1,0:T(1,128)} %bitcast.12, bf16[64,864]{1,0:T(8,128)(2,1)} %bitcast.8, f32[1,64]{1,0:T(1,128)} %bitcast.13), custom_call_target="tpu_custom_call" | custom-call | tf_op jit(solution)/shard_map/pallas_call | solution.py:450
  13.1 0.6 %copy.9 = bf16[3,1,1,4608]{3,0,2,1:T(4,128)(2,1)} copy(bf16[3,1,1,4608]{3,0,2,1:T(4,128)(2,1)S(1)} %bitcast.7) | data formatting | bytes 55296
